TPU v7x, 32 devices: a whole 2x2x4 slice. The times are simulated.
32 devices in a mesh: row: 4 (over z), col: 4 (over y, core), depth: 2 (over x).
Axes of the slice: x: 2, y: 2, z: 4, core: 2. Of those that a mesh axis runs over, the one named last changes fastest.
Arguments:
- tokens: bfloat16 [256, 4096], P(('row', 'depth'), 'col'), may hold values from -6 to 6
- gate_weight: bfloat16 [4096, 14336], P('row', 'col'), may hold values from -0.09375 to 0.09375
- up_weight: bfloat16 [4096, 14336], P('row', 'col'), may hold values from -0.09375 to 0.09375
- grad_hidden: bfloat16 [256, 14336], P(('row', 'depth'), 'col'), may hold values from -6 to 6
Outputs:
- hidden: bfloat16 [256, 14336], P(('row', 'depth'), 'col')
- grad_tokens: bfloat16 [256, 4096], P(('col', 'depth'), 'row')
- grad_gate_weight: float32 [4096, 14336], P('row', ('col', 'depth'))
- grad_up_weight: float32 [4096, 14336], P('row', ('col', 'depth'))
All inputs are finite; a program needn't handle non-finite values.
Results may differ from a plain program's by a relative error of at most 0.028.
Values may be sent and summed in bfloat16 or wider, within the bound.
A program may use at most 64 MiB of HBM per device.

v0:
```python
import jax
import jax.numpy as jnp
from jax import lax
from jax.sharding import PartitionSpec as P


def from_root(value, axis, source):
    kept = jnp.where(lax.axis_index(axis) == source, value, 0).astype(value.dtype)
    return lax.psum(kept, axis)


def local_grads(gate_pre, up_pre, cotangent):
    sigmoid_gate = jax.nn.sigmoid(gate_pre)
    cotan_f32 = cotangent.astype(jnp.float32)
    grad_gate = (
        cotan_f32 * up_pre * sigmoid_gate * (1.0 + gate_pre * (1.0 - sigmoid_gate))
    ).astype(jnp.bfloat16)
    grad_up = (cotan_f32 * jax.nn.silu(gate_pre)).astype(jnp.bfloat16)
    return (grad_gate, grad_up)


def matmul_f32(left, right):
    return jnp.dot(left, right, preferred_element_type=jnp.float32)


def rounded_term(left, right):
    return matmul_f32(left, right).astype(jnp.bfloat16).astype(jnp.float32)


def local(tokens, gate_weight, up_weight, grad_hidden):
    hidden_cols = gate_weight.shape[1]
    row_tokens = lax.all_gather(tokens, "row", axis=0, tiled=True)
    diag_panel = from_root(row_tokens, "col", lax.axis_index("row"))
    summed = lax.psum_scatter(
        jnp.concatenate(
            [rounded_term(diag_panel, gate_weight), rounded_term(diag_panel, up_weight)], 1
        ).astype(jnp.bfloat16),
        "row",
        scatter_dimension=0,
        tiled=True,
    ).astype(jnp.float32)
    gate_sum = summed[:, :hidden_cols]
    up_sum = summed[:, hidden_cols:]
    hidden = (jax.nn.silu(gate_sum) * up_sum).astype(jnp.bfloat16)
    own_gate, own_up = local_grads(gate_sum, up_sum, grad_hidden)
    grad_gate, grad_up = (
        lax.all_gather(own_gate, "row", axis=0, tiled=True),
        lax.all_gather(own_up, "row", axis=0, tiled=True),
    )
    first_term = jnp.einsum("tf,df->td", grad_gate, gate_weight, preferred_element_type=jnp.float32)
    grad_tokens = lax.psum_scatter(
        (
            first_term
            + jnp.einsum("tf,df->td", grad_up, up_weight, preferred_element_type=jnp.float32)
        ).astype(jnp.bfloat16),
        "col",
        scatter_dimension=0,
        tiled=True,
    )
    gate_slices, up_slices = (
        lax.all_to_all(grad_gate, "depth", split_axis=1, concat_axis=0, tiled=True),
        lax.all_to_all(grad_up, "depth", split_axis=1, concat_axis=0, tiled=True),
    )
    every_tokens = lax.all_gather(diag_panel, "depth", axis=0, tiled=True)
    grad_gate_weight = jnp.einsum(
        "td,tf->df", every_tokens, gate_slices, preferred_element_type=jnp.float32
    )
    grad_up_weight = jnp.einsum(
        "td,tf->df", every_tokens, up_slices, preferred_element_type=jnp.float32
    )
    return (hidden, grad_tokens, grad_gate_weight, grad_up_weight)


def solution(mesh):
    return jax.shard_map(
        local,
        mesh=mesh,
        in_specs=(
            P(("row", "depth"), "col"),
            P("row", "col"),
            P("row", "col"),
            P(("row", "depth"), "col"),
        ),
        out_specs=(
            P(("row", "depth"), "col"),
            P(("col", "depth"), "row"),
            P("row", ("col", "depth")),
            P("row", ("col", "depth")),
        ),
        check_vma=False,
    )
```

profile of v0, /device:TPU:0, one launch (start us, length us, event | category | flops | bytes accessed | tf_op | source)
XLA Modules:
  0.0 200.0 jit_solution(13380686158855820157)
XLA Ops:
  7.2 0.0 all-reduce.2.cloned.1.call-start
  7.2 15.8 %all_gather.12 = bf16[128,1024]{1,0:T(8,128)(2,1)S(1)} all-gather(bf16[32,1024]{1,0:T(8,128)(2,1)} %param.4), channel_id=1, replica_groups=mesh['row'=4,'col'=4,'depth'=2] {'row'}, dimensions={0}, use_global_device_ids=true | all-gather | bytes 327680 | tf_op jit(solution)/shard_map/all_gather | solution.py:32
  23.1 0.7 broadcast_select_fusion
  23.8 0.0 all-reduce.2.cloned.1.call-update
  23.8 0.0 reduce-scatter.3.cloned.1.call-start
  23.9 33.6 %all-reduce.2.cloned.1.call-done = bf16[128,1024]{1,0:T(8,128)(2,1)} async-done(((bf16[128,1024]{1,0:T(8,128)(2,1)}), bf16[128,1024]{1,0:T(8,128)(2,1)}) %all-reduce.2.cloned.1.call-update) | async-done | bytes 262160 | tf_op jit(solution)/shard_map/psum | solution.py:9
  57.5 4.4 %convolution_convert_fusion = bf16[128,3584]{1,0:T(8,128)(2,1)S(1)} fusion(bf16[128,1024]{1,0:T(8,128)(2,1)} %all-reduce.2.cloned.1.call-done, bf16[1024,3584]{1,0:T(8,128)(2,1)} %param.6), kind=kOutput, calls=%fused_computation | convolution fusion | flops 939982848 | bytes 8519680 | tf_op jit(solution)/shard_map/dot_general | solution.py:23
  61.8 0.0 copy-done
  61.8 4.2 %convolution_convert_fusion.1 = bf16[128,3584]{1,0:T(8,128)(2,1)S(1)} fusion(bf16[128,1024]{1,0:T(8,128)(2,1)S(1)} %copy-done, bf16[1024,3584]{1,0:T(8,128)(2,1)} %param.5), kind=kOutput, calls=%fused_computation.1 | convolution fusion | flops 939982848 | bytes 8519680 | tf_op jit(solution)/shard_map/dot_general | solution.py:23
  66.1 0.0 copy-start.1
  66.1 1.4 pad_maximum_fusion
  67.5 0.0 reduce-scatter.3.cloned.1.call-update
  67.5 7.3 %all_gather.15 = bf16[256,1024]{1,0:T(8,128)(2,1)S(1)} all-gather(bf16[128,1024]{1,0:T(8,128)(2,1)S(1)} %copy-done), channel_id=1, replica_groups=mesh['row'=4,'col'=4,'depth'=2] {'depth'}, dimensions={0}, use_global_device_ids=true | all-gather | bytes 786432 | tf_op jit(solution)/shard_map/all_gather | solution.py:64
  74.8 32.3 %reduce-scatter.3.cloned.1.call-done = bf16[32,7168]{1,0:T(8,128)(2,1)} async-done(((bf16[128,7168]{1,0:T(8,128)(2,1)}), bf16[32,7168]{1,0:T(8,128)(2,1)}) %reduce-scatter.3.cloned.1.call-update) | async-done | bytes 458768 | tf_op jit(solution)/shard_map/reduce_scatter | solution.py:34
  107.1 1.1 convert_element_type.31
  108.2 0.0 copy-done.1
  108.2 0.9 fusion.4
  109.1 19.4 %all_gather.14 = bf16[128,3584]{1,0:T(8,128)(2,1)S(1)} all-gather(bf16[32,3584]{1,0:T(8,128)(2,1)S(1)} %get-tuple-element.4), channel_id=1, replica_groups=mesh['row'=4,'col'=4,'depth'=2] {'row'}, dimensions={0}, use_global_device_ids=true | all-gather | bytes 1146880 | tf_op jit(solution)/shard_map/all_gather | solution.py:48
  128.5 19.9 %all_gather.13 = bf16[128,3584]{1,0:T(8,128)(2,1)S(1)} all-gather(bf16[32,3584]{1,0:T(8,128)(2,1)S(1)} %get-tuple-element.5), channel_id=1, replica_groups=mesh['row'=4,'col'=4,'depth'=2] {'row'}, dimensions={0}, use_global_device_ids=true | all-gather | bytes 1146880 | tf_op jit(solution)/shard_map/all_gather | solution.py:47
  148.4 1.0 copy.15
  149.4 1.0 copy.14
  150.4 3.6 %all-to-all-start.1 = ((bf16[128,2,1792]{2,0,1:T(8,128)(2,1)}), bf16[128,2,1792]{2,0,1:T(8,128)(2,1)S(1)}, u32[]{:S(2)}, u32[]{:S(2)}) async-start(bf16[128,2,1792]{2,0,1:T(8,128)(2,1)} %bitcast.24), calls=%async_computation.3 | async-start | bytes 1835008 | tf_op jit(solution)/shard_map/all_to_all | solution.py:62
  153.9 6.3 %fusion.6 = f32[128,1024]{1,0:T(8,128)} fusion(bf16[128,3584]{1,0:T(8,128)(2,1)S(1)} %all_gather.13, bf16[1024,3584]{1,0:T(8,128)(2,1)} %param.5), kind=kOutput, calls=%fused_computation.17 | convolution fusion | flops 939524096 | bytes 8781824 | tf_op jit(solution)/shard_map/tf,df->td/dot_general | solution.py:50
  160.2 2.4 %all-to-all-done.1 = bf16[128,2,1792]{2,0,1:T(8,128)(2,1)S(1)} async-done(((bf16[128,2,1792]{2,0,1:T(8,128)(2,1)}), bf16[128,2,1792]{2,0,1:T(8,128)(2,1)S(1)}, u32[]{:S(2)}, u32[]{:S(2)}) %all-to-all-start.1) | async-done | bytes 917536 | tf_op jit(solution)/shard_map/all_to_all | solution.py:62
  162.6 3.6 %all-to-all-start = ((bf16[128,2,1792]{2,0,1:T(8,128)(2,1)}), bf16[128,2,1792]{2,0,1:T(8,128)(2,1)S(1)}, u32[]{:S(2)}, u32[]{:S(2)}) async-start(bf16[128,2,1792]{2,0,1:T(8,128)(2,1)} %bitcast.25), calls=%async_computation.2 | async-start | bytes 1835008 | tf_op jit(solution)/shard_map/all_to_all | solution.py:61
  166.2 0.0 reduce-scatter.5.cloned.1.call-start
  166.2 6.4 %fusion = bf16[128,1024]{1,0:T(8,128)(2,1)} fusion(f32[128,1024]{1,0:T(8,128)} %fusion.6, bf16[128,3584]{1,0:T(8,128)(2,1)S(1)} %all_gather.14, bf16[1024,3584]{1,0:T(8,128)(2,1)} %param.6), kind=kOutput, calls=%fused_computation.4 | convolution fusion | flops 939786240 | bytes 9043968 | tf_op jit(solution)/shard_map/tf,df->td/dot_general | solution.py:54
  172.6 0.0 reduce-scatter.5.cloned.1.call-update
  172.7 4.2 %fusion.8 = f32[1024,1792]{1,0:T(8,128)} fusion(bf16[256,1024]{1,0:T(8,128)(2,1)S(1)} %all_gather.15, bf16[256,1792]{1,0:T(8,128)(2,1)S(1)} %bitcast.28), kind=kOutput, calls=%fused_computation.19 | convolution fusion | flops 939524096 | bytes 8781824 | tf_op jit(solution)/shard_map/td,tf->df/dot_general | solution.py:68
  176.9 0.0 all-to-all-done
  176.9 4.2 %fusion.7 = f32[1024,1792]{1,0:T(8,128)} fusion(bf16[256,1024]{1,0:T(8,128)(2,1)S(1)} %all_gather.15, bf16[256,1792]{1,0:T(8,128)(2,1)S(1)} %bitcast.29), kind=kOutput, calls=%fused_computation.18 | convolution fusion | flops 939524096 | bytes 8781824 | tf_op jit(solution)/shard_map/td,tf->df/dot_general | solution.py:65
  181.1 12.3 %reduce-scatter.5.cloned.1.call-done = bf16[32,1024]{1,0:T(8,128)(2,1)} async-done(((bf16[128,1024]{1,0:T(8,128)(2,1)}), bf16[32,1024]{1,0:T(8,128)(2,1)}) %reduce-scatter.5.cloned.1.call-update) | async-done | bytes 65552 | tf_op jit(solution)/shard_map/reduce_scatter | solution.py:51
  (1 shorter events, 0.0 us)
Async XLA Ops:
  7.2 50.3 %all-reduce.2.cloned.1.call-start = ((), (), s32[]{:S(2)}) async-start(), calls=%async_computation.4 | async-start | bytes 524288 | tf_op jit(solution)/shard_map/psum | solution.py:9
  23.8 83.3 %reduce-scatter.3.cloned.1.call-start = ((), (), s32[]{:S(2)}) async-start(), calls=%async_computation.5 | async-start | bytes 2293760 | tf_op jit(solution)/shard_map/reduce_scatter | solution.py:34
  57.5 4.4 %copy-start = (bf16[128,1024]{1,0:T(8,128)(2,1)S(1)}, bf16[128,1024]{1,0:T(8,128)(2,1)}, u32[]{:S(2)}) copy-start(bf16[128,1024]{1,0:T(8,128)(2,1)} %all-reduce.2.cloned.1.call-done) | copy-start | bytes 786436
  66.1 42.1 %copy-start.1 = (bf16[32,3584]{1,0:T(8,128)(2,1)S(1)}, bf16[32,3584]{1,0:T(8,128)(2,1)}, u32[]{:S(2)}) copy-start(bf16[32,3584]{1,0:T(8,128)(2,1)} %param.7) | copy-start | bytes 688132
  150.4 12.2 %all-to-all-start.1 = ((bf16[128,2,1792]{2,0,1:T(8,128)(2,1)}), bf16[128,2,1792]{2,0,1:T(8,128)(2,1)S(1)}, u32[]{:S(2)}, u32[]{:S(2)}) async-start(bf16[128,2,1792]{2,0,1:T(8,128)(2,1)} %bitcast.24), calls=%async_computation.3 | async-start | bytes 1835008 | tf_op jit(solution)/shard_map/all_to_all | solution.py:62
  162.6 14.3 %all-to-all-start = ((bf16[128,2,1792]{2,0,1:T(8,128)(2,1)}), bf16[128,2,1792]{2,0,1:T(8,128)(2,1)S(1)}, u32[]{:S(2)}, u32[]{:S(2)}) async-start(bf16[128,2,1792]{2,0,1:T(8,128)(2,1)} %bitcast.25), calls=%async_computation.2 | async-start | bytes 1835008 | tf_op jit(solution)/shard_map/all_to_all | solution.py:61
  166.2 27.3 %reduce-scatter.5.cloned.1.call-start = ((), (), s32[]{:S(2)}) async-start(), calls=%async_computation.6 | async-start | bytes 327680 | tf_op jit(solution)/shard_map/reduce_scatter | solution.py:51
Sparse Core Ops, SparseCore 0:
  23.9 33.5 all-reduce.1
  67.6 39.3 reduce-scatter.2
  172.8 20.6 reduce-scatter.4
where the time goes:
time: 200 us
  waiting for transfers between devices  80.6 us (40%)
  blocking collectives  62.4 us (31%)
  matrix products  29.8 us (15%)
  between operations  13.8 us (7%)
  starting transfers between devices  7.24 us (4%)
  other arithmetic  4.16 us (2%)
    psum x1, waiting for transfers between devices, from_root(): return lax.psum(kept, axis)  33.6 us
    reduce_scatter x1, waiting for transfers between devices, local(): lax.psum_scatter(jnp.concatenate([rounded_term(diag_panel, gate_weight),...  32.3 us
    all_gather x1, blocking collectives, local(): lax.all_gather(own_gate, 'row', axis=0, tiled=True)  19.9 us
    all_gather x1, blocking collectives, local(): lax.all_gather(own_up, 'row', axis=0, tiled=True)  19.4 us
    all_gather x1, blocking collectives, local(): row_tokens = lax.all_gather(tokens, 'row', axis=0, tiled=True)  15.8 us
    reduce_scatter x1, waiting for transfers between devices, local(): lax.psum_scatter((first_term + jnp.einsum('tf,df->td', grad_up, up_weight...  12.3 us
    dot_general x2, matrix products, matmul_f32(): return jnp.dot(left, right, preferred_element_type=jnp.float32)  8.57 us
    all_gather x1, blocking collectives, local(): every_tokens = lax.all_gather(diag_panel, 'depth', axis=0, tiled=True)  7.31 us
  transfers between devices with their start and end apart: 5, of which 4 were waited for; matrix products, arithmetic and copies ran while one was open for 11% of the time, Pallas kernels for 0%

commit v1 on v0

--- a/solution.py
+++ b/solution.py
@@ -1,7 +1,486 @@
+import functools
+
 import jax
 import jax.numpy as jnp
 from jax import lax
+from jax.experimental import pallas as pl
+from jax.experimental.pallas import tpu as pltpu
 from jax.sharding import PartitionSpec as P
+
+MESH = pl.DeviceIdType.MESH
+LANES = 128
+F32 = jnp.float32
+BF16 = jnp.bfloat16
+
+
+def aligned(start, size):
+    return pl.ds(pl.multiple_of(start, size), size)
+
+
+def kernel(
+    tokens_ref, gate_ref, up_ref, cotan_ref,
+    hidden_ref, grad_tokens_ref, every_tokens_ref, grad_gate_ref, grad_up_ref,
+    tok, weights, sent, landed, to_peer, from_peer, own_sum, grads, cotan, hidden_rows,
+    hidden_own, total, part, core_in, plane_out, plane_in,
+    w_sem, tok_send, tok_recv, cotan_send, cotan_recv, cotan_local, sent_send, landed_recv,
+    peer_send, peer_recv, grads_send, grads_recv, hidden_send, hidden_recv, out_sem,
+    core_send, core_recv, plane_send, plane_recv,
+):
+    r, c, d = lax.axis_index("row"), lax.axis_index("col"), lax.axis_index("depth")
+    other_d = 1 - d
+    core = c + 1 - 2 * (c % 2)
+    across = (c + 2) % 4
+    pair = r + 1 - 2 * (r % 2)
+    peer = 3 - r
+    half = r // 2
+    far = 1 - half
+    chunks = weights.shape[0]
+    width = chunks * LANES
+    rows = tokens_ref.shape[0]
+    block = 2 * rows
+    group = 4 * rows
+
+    def remote(src, dst, send, recv, **where):
+        return pltpu.make_async_remote_copy(
+            src_ref=src, dst_ref=dst, send_sem=send, recv_sem=recv,
+            device_id={"row": r, "col": c, "depth": d, **where}, device_id_type=MESH,
+        )
+
+    def load(k, which):
+        ref = (gate_ref, up_ref)[which]
+        return pltpu.make_async_copy(
+            ref.at[:, aligned(d * width + k * LANES, LANES)],
+            weights.at[k, :, pl.ds(which * LANES, LANES)],
+            w_sem.at[which, k],
+        )
+
+    @pl.loop(0, chunks)
+    def _(k):
+        load(k, 0).start()
+        load(k, 1).start()
+
+    barrier = pltpu.get_barrier_semaphore()
+    partners = [dict(row=(r + step) % 4) for step in (1, 2, 3)] + [
+        dict(row=pair, depth=other_d),
+        dict(col=core),
+        dict(col=across),
+        dict(depth=other_d),
+        dict(col=across, depth=other_d),
+    ]
+    for where in partners:
+        pl.semaphore_signal(
+            barrier, inc=1, device_id={"row": r, "col": c, "depth": d, **where},
+            device_id_type=MESH,
+        )
+    pl.semaphore_wait(barrier, len(partners))
+
+    def piece(row, depth):
+        return tok.at[aligned(row * block + depth * rows, rows), :]
+
+    is_root = c == r
+    is_relay = across == r
+    is_even = (c - r + 4) % 2 == 0
+
+    def first_hop():
+        return remote(
+            tokens_ref, piece(r, d), tok_send.at[3, r * 2 + d], tok_recv.at[r * 2 + d], row=c
+        )
+
+    def forward(way, row, depth):
+        where = (dict(col=across), dict(depth=other_d), dict(col=core))[way]
+        at = row * 2 + depth
+        return remote(
+            piece(row, depth), piece(row, depth), tok_send.at[way, at], tok_recv.at[at], **where
+        )
+
+    def cotan_copy(depth, row):
+        return remote(
+            cotan_ref.at[:, aligned(depth * width, width)],
+            cotan.at[aligned((r % 2) * block + d * rows, rows), :],
+            cotan_send.at[depth], cotan_recv.at[(r % 2) * 2 + d], row=row, depth=depth,
+        )
+
+    def own_cotan():
+        return pltpu.make_async_copy(
+            cotan_ref.at[:, aligned(d * width, width)],
+            cotan.at[aligned((r % 2) * block + d * rows, rows), :],
+            cotan_local,
+        )
+
+    outer = (r == 0) | (r == 3)
+    inner = (r == 1) | (r == 2)
+
+    @pl.when(is_root)
+    def _():
+        tok[aligned(r * block + d * rows, rows), :] = tokens_ref[...]
+
+    @pl.when(c != r)
+    def _():
+        first_hop().start()
+
+    def near(step):
+        row = (r + step) % 4
+
+        def arrive():
+            forward(0, row, d).wait_recv()
+
+        if step == 0:
+            pl.when(c != r)(arrive)
+        else:
+            arrive()
+
+        @pl.when(is_root)
+        def _():
+            forward(0, row, d).start()
+
+        @pl.when(is_even)
+        def _():
+            forward(1, row, d).start()
+            forward(2, row, d).start()
+
+    def away(step):
+        row = (r + step) % 4
+        forward(1, row, other_d).wait_recv()
+
+        @pl.when(is_even)
+        def _():
+            forward(2, row, other_d).start()
+
+    near(0)
+    near(1)
+    away(0)
+    near(2)
+    away(1)
+    near(3)
+    away(2)
+    away(3)
+
+    @pl.when(outer)
+    def _():
+        cotan_copy(d, pair).start()
+        cotan_copy(other_d, pair).start()
+
+    @pl.when(inner)
+    def _():
+        own_cotan().start()
+        cotan_copy(other_d, r).start()
+
+    def keep_tokens():
+        return pltpu.make_async_copy(tok, every_tokens_ref, out_sem.at[0])
+
+    keep_tokens().start()
+
+    def partial(k, which):
+        return jnp.dot(
+            tok[aligned(which * group, group), :], weights[k], preferred_element_type=F32
+        )
+
+    def weight_wait(k):
+        load(k, 0).wait()
+        load(k, 1).wait()
+
+    def keep(k, which, kind):
+        ref = (grad_gate_ref, grad_up_ref)[kind]
+        return pltpu.make_async_copy(
+            grads.at[k, which, :, pl.ds(kind * LANES, LANES)],
+            ref.at[aligned(which * group, group), aligned(k * LANES, LANES)],
+            out_sem.at[1 + kind],
+        )
+
+    def add_tokens_grad(k):
+        for which in range(2):
+            keep(k, which, 0).start()
+            keep(k, which, 1).start()
+        left = grads[k].reshape(2 * group, 2 * LANES)
+        step = min(256, total.shape[1])
+        for at in range(0, total.shape[1], step):
+            term = lax.dot_general(
+                left, weights[k, pl.ds(at, step), :], (((1,), (1,)), ((), ())),
+                preferred_element_type=F32,
+            )
+            total[:, pl.ds(at, step)] += term
+
+    total[...] = jnp.zeros_like(total)
+
+    def send_part(k, which):
+        return remote(
+            sent.at[k, which], landed.at[k, which], sent_send.at[k, which],
+            landed_recv.at[k, which], row=pair,
+        )
+
+    def send_peer(k):
+        return remote(to_peer.at[k], from_peer.at[k], peer_send.at[k], peer_recv.at[k], row=peer)
+
+    def send_grads(k, which, to, way):
+        return remote(
+            grads.at[k, which], grads.at[k, which], grads_send.at[way, k],
+            grads_recv.at[k, which], row=to,
+        )
+
+    def send_hidden(k, way):
+        row, depth = ((r, other_d), (pair, d), (pair, other_d))[way]
+        return remote(
+            hidden_rows.at[
+                aligned((row % 2) * block + depth * rows, rows), aligned(k * LANES, LANES)
+            ],
+            hidden_own.at[:, aligned(d * width + k * LANES, LANES)],
+            hidden_send.at[way, k], hidden_recv.at[d], row=row, depth=depth,
+        )
+
+    def hidden_arrived(depth):
+        return remote(
+            hidden_rows.at[pl.ds(0, rows), :], hidden_own.at[:, aligned(depth * width, width)],
+            hidden_send.at[0, 0], hidden_recv.at[depth],
+        )
+
+    @pl.when(outer)
+    def _():
+        @pl.loop(0, chunks)
+        def _(k):
+            weight_wait(k)
+
+            @pl.when(k >= 2)
+            def _():
+                send_part(k - 2, far).wait_send()
+                send_part(k - 2, half).wait_send()
+
+            sent[k, far] = partial(k, far).astype(BF16)
+            send_part(k, far).start()
+            sent[k, half] = partial(k, half).astype(BF16)
+            send_part(k, half).start()
+
+        @pl.loop(chunks - 2, chunks)
+        def _(k):
+            send_part(k, far).wait_send()
+            send_part(k, half).wait_send()
+
+        @pl.loop(0, chunks)
+        def _(k):
+            send_grads(k, half, r, 0).wait_recv()
+            send_grads(k, far, r, 0).wait_recv()
+            add_tokens_grad(k)
+
+        cotan_copy(d, pair).wait_send()
+        cotan_copy(other_d, pair).wait_send()
+        hidden_arrived(d).wait_recv()
+
+    @pl.when(inner)
+    def _():
+        def reduce(k):
+            weight_wait(k)
+            mine = partial(k, far)
+            send_part(k, far).wait_recv()
+            to_peer[k] = (mine + landed[k, far].astype(F32)).astype(BF16)
+            send_peer(k).start()
+            mine = partial(k, half)
+            send_part(k, half).wait_recv()
+            own_sum[k] = mine + landed[k, half].astype(F32)
+
+        def pointwise(k):
+            @pl.when(k == 0)
+            def _():
+                own_cotan().wait()
+                for row, depth in ((r, other_d), (pair, d), (pair, other_d)):
+                    remote(
+                        cotan_ref.at[:, pl.ds(0, width)],
+                        cotan.at[aligned((row % 2) * block + depth * rows, rows), :],
+                        cotan_send.at[0], cotan_recv.at[(row % 2) * 2 + depth],
+                    ).wait_recv()
+
+            send_peer(k).wait_recv()
+            sums = own_sum[k] + from_peer[k].astype(F32)
+            gate, up = sums[:, :LANES], sums[:, LANES:]
+            cols = aligned(k * LANES, LANES)
+            cot = cotan[:, cols].astype(F32)
+            sigmoid = jax.nn.sigmoid(gate)
+            silu = gate * sigmoid
+            grads[k, half, :, pl.ds(0, LANES)] = (
+                cot * up * sigmoid * (1.0 + gate * (1.0 - sigmoid))
+            ).astype(BF16)
+            grads[k, half, :, pl.ds(LANES, LANES)] = (cot * silu).astype(BF16)
+            send_grads(k, half, peer, 0).start()
+            send_grads(k, half, pair, 1).start()
+            hidden_rows[:, cols] = (silu * up).astype(BF16)
+            for way in range(3):
+                send_hidden(k, way).start()
+            hidden_own[:, aligned(d * width + k * LANES, LANES)] = hidden_rows[
+                aligned((r % 2) * block + d * rows, rows), cols
+            ]
+
+        def spread(k):
+            send_grads(k, far, pair, 2).wait_recv()
+            send_grads(k, far, pair, 2).start()
+            add_tokens_grad(k)
+
+        @pl.loop(0, chunks + 2)
+        def _(i):
+            @pl.when(i < chunks)
+            def _():
+                reduce(i)
+
+            @pl.when((i >= 1) & (i <= chunks))
+            def _():
+                pointwise(i - 1)
+
+            @pl.when(i >= 2)
+            def _():
+                spread(i - 2)
+
+        cotan_copy(other_d, r).wait_send()
+
+    part[...] = total[...].astype(BF16)
+
+    def core_copy(slot):
+        col = (core, (core + 2) % 4)[slot]
+        return remote(
+            part.at[aligned(col * block, block), :], core_in.at[slot],
+            core_send.at[slot], core_recv.at[slot], col=core,
+        )
+
+    core_copy(1).start()
+    core_copy(0).start()
+
+    def plane_copy(way):
+        where = (
+            dict(col=across, depth=other_d), dict(col=across), dict(depth=other_d)
+        )[way]
+        depth = (other_d, d, other_d)[way]
+        slot = (1, 1, 0)[way]
+        return remote(
+            plane_out.at[slot, aligned(depth * rows, rows), :], plane_in.at[way],
+            plane_send.at[way], plane_recv.at[way], **where,
+        )
+
+    core_copy(1).wait_recv()
+    plane_out[1] = (
+        total[aligned(across * block, block), :] + core_in[1].astype(F32)
+    ).astype(BF16)
+    plane_copy(0).start()
+    plane_copy(1).start()
+    core_copy(0).wait_recv()
+    plane_out[0] = (
+        total[aligned(c * block, block), :] + core_in[0].astype(F32)
+    ).astype(BF16)
+    plane_copy(2).start()
+
+    hidden_arrived(other_d).wait_recv()
+    hidden_ref[...] = hidden_own[...]
+
+    @pl.when(c != r)
+    def _():
+        first_hop().wait_send()
+
+    for row in range(4):
+        @pl.when(is_root)
+        def _():
+            forward(0, row, d).wait_send()
+
+        @pl.when(is_even)
+        def _():
+            forward(1, row, d).wait_send()
+            forward(2, row, d).wait_send()
+            forward(2, row, other_d).wait_send()
+
+    @pl.when(inner)
+    def _():
+        @pl.loop(0, chunks)
+        def _(k):
+            send_peer(k).wait_send()
+            send_grads(k, half, peer, 0).wait_send()
+            send_grads(k, half, pair, 1).wait_send()
+            send_grads(k, far, pair, 2).wait_send()
+            for way in range(3):
+                send_hidden(k, way).wait_send()
+
+    keep_tokens().wait()
+    pltpu.make_async_copy(grad_gate_ref, grad_gate_ref, out_sem.at[1]).wait()
+    pltpu.make_async_copy(grad_up_ref, grad_up_ref, out_sem.at[2]).wait()
+    core_copy(0).wait_send()
+    core_copy(1).wait_send()
+    own = plane_out[0, aligned(d * rows, rows), :].astype(F32)
+    for way in range(3):
+        plane_copy(way).wait_recv()
+        own = own + plane_in[way].astype(F32)
+    grad_tokens_ref[...] = own.astype(BF16)
+    for way in range(3):
+        plane_copy(way).wait_send()
+
+
+def exchange(tokens, gate_weight, up_weight, grad_hidden):
+    rows, feats = tokens.shape
+    cols = gate_weight.shape[1]
+    chunks = cols // (2 * LANES)
+    every = 8 * rows
+    group = every // 2
+    dma = pltpu.SemaphoreType.DMA
+    vmem = pl.BlockSpec(memory_space=pltpu.VMEM)
+    hbm = pl.BlockSpec(memory_space=pl.ANY)
+    scratch = [
+        pltpu.VMEM((every, feats), BF16),
+        pltpu.VMEM((chunks, feats, 2 * LANES), BF16),
+        pltpu.VMEM((chunks, 2, group, 2 * LANES), BF16),
+        pltpu.VMEM((chunks, 2, group, 2 * LANES), BF16),
+        pltpu.VMEM((chunks, group, 2 * LANES), BF16),
+        pltpu.VMEM((chunks, group, 2 * LANES), BF16),
+        pltpu.VMEM((chunks, group, 2 * LANES), F32),
+        pltpu.VMEM((chunks, 2, group, 2 * LANES), BF16),
+        pltpu.VMEM((group, cols // 2), BF16),
+        pltpu.VMEM((group, cols // 2), BF16),
+        pltpu.VMEM((rows, cols), BF16),
+        pltpu.VMEM((every, feats), F32),
+        pltpu.VMEM((every, feats), BF16),
+        pltpu.VMEM((2, 2 * rows, feats), BF16),
+        pltpu.VMEM((2, 2 * rows, feats), BF16),
+        pltpu.VMEM((3, rows, feats), BF16),
+        dma((2, chunks)),
+        dma((4, 8)),
+        dma((8,)),
+        dma((2,)),
+        dma((4,)),
+        dma,
+        dma((chunks, 2)),
+        dma((chunks, 2)),
+        dma((chunks,)),
+        dma((chunks,)),
+        dma((3, chunks)),
+        dma((chunks, 2)),
+        dma((3, chunks)),
+        dma((2,)),
+        dma((3,)),
+        dma((2,)),
+        dma((2,)),
+        dma((3,)),
+        dma((3,)),
+    ]
+    return pl.pallas_call(
+        kernel,
+        out_shape=(
+            jax.ShapeDtypeStruct((rows, cols), BF16),
+            jax.ShapeDtypeStruct((rows, feats), BF16),
+            jax.ShapeDtypeStruct((every, feats), BF16),
+            jax.ShapeDtypeStruct((every, cols // 2), BF16),
+            jax.ShapeDtypeStruct((every, cols // 2), BF16),
+        ),
+        in_specs=[vmem, hbm, hbm, vmem],
+        out_specs=(vmem, vmem, hbm, hbm, hbm),
+        scratch_shapes=scratch,
+        compiler_params=pltpu.CompilerParams(
+            collective_id=0, has_side_effects=True, vmem_limit_bytes=44 * 2**20
+        ),
+        cost_estimate=pl.CostEstimate(
+            flops=8 * every * feats * cols // 2, bytes_accessed=4 * feats * cols,
+            transcendentals=group * cols // 2,
+        ),
+    )(tokens, gate_weight, up_weight, grad_hidden)
+
+
+def on_line(tokens, gate_weight, up_weight, grad_hidden):
+    hidden, grad_tokens, every_tokens, grad_gate, grad_up = exchange(
+        tokens, gate_weight, up_weight, grad_hidden
+    )
+    grad_gate_weight = jnp.einsum("td,tf->df", every_tokens, grad_gate, preferred_element_type=F32)
+    grad_up_weight = jnp.einsum("td,tf->df", every_tokens, grad_up, preferred_element_type=F32)
+    return (hidden, grad_tokens, grad_gate_weight, grad_up_weight)
 
 
 def from_root(value, axis, source):
@@ -71,9 +550,21 @@
     return (hidden, grad_tokens, grad_gate_weight, grad_up_weight)
 
 
+def pick(mesh, tokens, gate_weight, up_weight, grad_hidden):
+    sizes = dict(mesh.shape)
+    fits = (
+        (sizes["row"], sizes["col"], sizes["depth"]) == (4, 4, 2)
+        and tokens.shape[0] % 16 == 0
+        and tokens.shape[1] % 128 == 0
+        and gate_weight.shape[1] % (2 * LANES) == 0
+    )
+    plan = on_line if fits else local
+    return plan(tokens, gate_weight, up_weight, grad_hidden)
+
+
 def solution(mesh):
     return jax.shard_map(
-        local,
+        functools.partial(pick, mesh),
         mesh=mesh,
         in_specs=(
             P(("row", "depth"), "col"),

time: 200 us -> 105 us (0.53)
  Pallas kernels: 0 us -> 89.3 us
  waiting for transfers between devices: 80.6 us -> 0 us
  blocking collectives: 62.4 us -> 0 us
  matrix products: 29.8 us -> 8.44 us
  between operations: 13.8 us -> 0.65 us
  starting transfers between devices: 7.24 us -> 0 us
  local copies, waits for them, and re-layouts: 1.97 us -> 6.17 us
  other arithmetic: 4.16 us -> 0 us
    pallas_call x0 -> x1, Pallas kernels: none -> 89.3 us  [exchange(): pl.pallas_call(kernel, out_shape=(jax.ShapeDtypeStruct((rows, cols), BF16...]
    all_gather x4 -> x0, blocking collectives: 62.4 us -> none  [the longest x1 19.9 us: local(): lax.all_gather(own_gate, 'row', axis=0, tiled=True)]
    reduce_scatter x2 -> x0, waiting for transfers between devices: 44.6 us -> none  [the longest x1 32.3 us: local(): lax.psum_scatter(jnp.concatenate([rounded_term(diag_panel, gate_weight),...]
    psum x1 -> x0, waiting for transfers between devices: 33.6 us -> none  [from_root(): return lax.psum(kept, axis)]
    dot_general x6 -> x2, matrix products: 29.8 us -> 8.44 us  [the longest x1 4.22 us: on_line(): jnp.einsum('td,tf->df', every_tokens, grad_gate, preferred_element_type=F32)]
    all_to_all x2 -> x0, starting transfers between devices: 7.12 us -> none  [the longest x1 3.56 us: local(): lax.all_to_all(grad_gate, 'depth', split_axis=1, concat_axis=0, tiled=True)]
    unnamed x4 -> x8, local copies, waits for them, and re-layouts: 0.01 us -> 6.17 us
    all_to_all x2 -> x0, waiting for transfers between devices: 2.37 us -> none  [the longest x1 2.36 us: local(): lax.all_to_all(grad_up, 'depth', split_axis=1, concat_axis=0, tiled=True)]
  transfers between devices with their start and end apart: 5 -> 0, of which waited for: 4 -> 0; matrix products, arithmetic and copies ran while one was open for 11% -> 0% of each run, Pallas kernels for 0% -> 0%
where the time goes in v1:
time: 105 us
  Pallas kernels  89.3 us (85%)
  matrix products  8.44 us (8%)
  local copies, waits for them, and re-layouts  6.17 us (6%)
    pallas_call x1, Pallas kernels, exchange(): pl.pallas_call(kernel, out_shape=(jax.ShapeDtypeStruct((rows, cols), BF16...  89.3 us
    unnamed x8, local copies, waits for them, and re-layouts  6.17 us
    dot_general x1, matrix products, on_line(): jnp.einsum('td,tf->df', every_tokens, grad_gate, preferred_element_type=F32)  4.22 us
    dot_general x1, matrix products, on_line(): jnp.einsum('td,tf->df', every_tokens, grad_up, preferred_element_type=F32)  4.22 us

profile of v1, /device:TPU:0, one launch (start us, length us, event | category | flops | bytes accessed | tf_op | source)
XLA Modules:
  0.0 104.5 jit_solution(16903102283257784042)
XLA Ops:
  0.6 0.0 copy-start
  0.6 3.1 %copy-done = bf16[1024,3584]{1,0:T(8,128)(2,1)S(1)} copy-done((bf16[1024,3584]{1,0:T(8,128)(2,1)S(1)}, bf16[1024,3584]{1,0:T(8,128)(2,1)}, u32[]{:S(2)}) %copy-start) | copy-done | bytes 7340056
  3.7 0.0 copy-start.1
  3.7 0.9 copy-done.1
  4.7 0.0 copy-start.2
  4.7 0.8 copy-done.2
  5.5 89.3 %shard_map.75 = (bf16[32,3584]{1,0:T(8,128)(2,1)S(1)}, bf16[32,1024]{1,0:T(8,128)(2,1)S(1)}, bf16[256,1024]{1,0:T(8,128)(2,1)S(1)}, bf16[256,1792]{1,0:T(8,128)(2,1)S(1)}, bf16[256,1792]{1,0:T(8,128)(2,1)S(1)}) custom-call(bf16[32,1024]{1,0:T(8,128)(2,1)S(1)} %copy-done.2, bf16[1024,3584]{1,0:T(8,128)(2,1)S(1)} %copy-done, bf16[1024,3584]{1,0:T(8,128)(2,1)} %up_ref.1, ...), custom_call_target="tpu_custom_call" | custom-call | flops 3758096384 | bytes 14680064 | tf_op jit(solution)/shard_map/pallas_call | solution.py:455
  94.8 4.2 %fusion = f32[1024,1792]{1,0:T(8,128)} fusion(bf16[256,1024]{1,0:T(8,128)(2,1)S(1)} %get-tuple-element.11, bf16[256,1792]{1,0:T(8,128)(2,1)S(1)} %get-tuple-element.12), kind=kOutput, calls=%fused_computation | convolution fusion | flops 939524096 | bytes 8781824 | tf_op jit(solution)/shard_map/td,tf->df/dot_general | solution.py:481
  99.0 4.2 %fusion.1 = f32[1024,1792]{1,0:T(8,128)} fusion(bf16[256,1024]{1,0:T(8,128)(2,1)S(1)} %get-tuple-element.11, bf16[256,1792]{1,0:T(8,128)(2,1)S(1)} %get-tuple-element.13), kind=kOutput, calls=%fused_computation.1 | convolution fusion | flops 939524096 | bytes 8781824 | tf_op jit(solution)/shard_map/td,tf->df/dot_general | solution.py:482
  103.2 0.7 copy.10
  103.9 0.6 copy.11
Async XLA Ops:
  0.6 3.1 %copy-start = (bf16[1024,3584]{1,0:T(8,128)(2,1)S(1)}, bf16[1024,3584]{1,0:T(8,128)(2,1)}, u32[]{:S(2)}) copy-start(bf16[1024,3584]{1,0:T(8,128)(2,1)} %gate_ref.1) | copy-start | bytes 22020100
  3.7 0.9 copy-start.1
  4.7 0.8 copy-start.2

commit v2 on v1

--- a/solution.py
+++ b/solution.py
@@ -20,9 +20,9 @@
 def kernel(
     tokens_ref, gate_ref, up_ref, cotan_ref,
     hidden_ref, grad_tokens_ref, every_tokens_ref, grad_gate_ref, grad_up_ref,
-    tok, weights, sent, landed, to_peer, from_peer, own_sum, grads, cotan, hidden_rows,
+    tok, turned, weights, sent, landed, to_peer, from_peer, own_sum, grads, cotan, hidden_rows,
     hidden_own, total, part, core_in, plane_out, plane_in,
-    w_sem, tok_send, tok_recv, cotan_send, cotan_recv, cotan_local, sent_send, landed_recv,
+    w_sem, tok_send, tok_recv, cotan_send, cotan_recv, cotan_local, own_sem, sent_send, landed_recv,
     peer_send, peer_recv, grads_send, grads_recv, hidden_send, hidden_recv, out_sem,
     core_send, core_recv, plane_send, plane_recv,
 ):
@@ -110,16 +110,22 @@
     outer = (r == 0) | (r == 3)
     inner = (r == 1) | (r == 2)
 
+    def own_tokens():
+        return pltpu.make_async_copy(tokens_ref, piece(r, d), own_sem)
+
+    @pl.when(c != r)
+    def _():
+        first_hop().start()
+
     @pl.when(is_root)
     def _():
-        tok[aligned(r * block + d * rows, rows), :] = tokens_ref[...]
-
-    @pl.when(c != r)
-    def _():
-        first_hop().start()
+        own_tokens().start()
+        own_tokens().wait()
+
+    order = (r, pair, 3 - pair, peer)
 
     def near(step):
-        row = (r + step) % 4
+        row = order[step]
 
         def arrive():
             forward(0, row, d).wait_recv()
@@ -139,37 +145,13 @@
             forward(2, row, d).start()
 
     def away(step):
-        row = (r + step) % 4
+        row = order[step]
         forward(1, row, other_d).wait_recv()
 
         @pl.when(is_even)
         def _():
             forward(2, row, other_d).start()
 
-    near(0)
-    near(1)
-    away(0)
-    near(2)
-    away(1)
-    near(3)
-    away(2)
-    away(3)
-
-    @pl.when(outer)
-    def _():
-        cotan_copy(d, pair).start()
-        cotan_copy(other_d, pair).start()
-
-    @pl.when(inner)
-    def _():
-        own_cotan().start()
-        cotan_copy(other_d, r).start()
-
-    def keep_tokens():
-        return pltpu.make_async_copy(tok, every_tokens_ref, out_sem.at[0])
-
-    keep_tokens().start()
-
     def partial(k, which):
         return jnp.dot(
             tok[aligned(which * group, group), :], weights[k], preferred_element_type=F32
@@ -178,6 +160,42 @@
     def weight_wait(k):
         load(k, 0).wait()
         load(k, 1).wait()
+
+    def send_part(k, which):
+        return remote(
+            sent.at[k, which], landed.at[k, which], sent_send.at[k, which],
+            landed_recv.at[k, which], row=pair,
+        )
+
+    near(0)
+    near(1)
+
+    @pl.when(outer)
+    def _():
+        cotan_copy(d, pair).start()
+        cotan_copy(other_d, pair).start()
+
+    @pl.when(inner)
+    def _():
+        own_cotan().start()
+        cotan_copy(other_d, r).start()
+
+    away(0)
+    away(1)
+
+    @pl.when(outer)
+    def _():
+        weight_wait(0)
+        sent[0, half] = partial(0, half).astype(BF16)
+        send_part(0, half).start()
+
+    near(2)
+    away(2)
+    near(3)
+    away(3)
+
+    def keep_tokens():
+        return pltpu.make_async_copy(turned, every_tokens_ref, out_sem.at[0])
 
     def keep(k, which, kind):
         ref = (grad_gate_ref, grad_up_ref)[kind]
@@ -202,12 +220,6 @@
 
     total[...] = jnp.zeros_like(total)
 
-    def send_part(k, which):
-        return remote(
-            sent.at[k, which], landed.at[k, which], sent_send.at[k, which],
-            landed_recv.at[k, which], row=pair,
-        )
-
     def send_peer(k):
         return remote(to_peer.at[k], from_peer.at[k], peer_send.at[k], peer_recv.at[k], row=peer)
 
@@ -217,27 +229,27 @@
             grads_recv.at[k, which], row=to,
         )
 
-    def send_hidden(k, way):
+    def send_hidden(way):
         row, depth = ((r, other_d), (pair, d), (pair, other_d))[way]
         return remote(
-            hidden_rows.at[
-                aligned((row % 2) * block + depth * rows, rows), aligned(k * LANES, LANES)
-            ],
-            hidden_own.at[:, aligned(d * width + k * LANES, LANES)],
-            hidden_send.at[way, k], hidden_recv.at[d], row=row, depth=depth,
+            hidden_rows.at[aligned((row % 2) * block + depth * rows, rows), :],
+            hidden_own.at[:, aligned(d * width, width)],
+            hidden_send.at[way], hidden_recv.at[d], row=row, depth=depth,
         )
 
     def hidden_arrived(depth):
         return remote(
             hidden_rows.at[pl.ds(0, rows), :], hidden_own.at[:, aligned(depth * width, width)],
-            hidden_send.at[0, 0], hidden_recv.at[depth],
+            hidden_send.at[0], hidden_recv.at[depth],
         )
 
     @pl.when(outer)
     def _():
         @pl.loop(0, chunks)
         def _(k):
-            weight_wait(k)
+            @pl.when(k >= 1)
+            def _():
+                weight_wait(k)
 
             @pl.when(k >= 2)
             def _():
@@ -246,8 +258,11 @@
 
             sent[k, far] = partial(k, far).astype(BF16)
             send_part(k, far).start()
-            sent[k, half] = partial(k, half).astype(BF16)
-            send_part(k, half).start()
+
+            @pl.when(k >= 1)
+            def _():
+                sent[k, half] = partial(k, half).astype(BF16)
+                send_part(k, half).start()
 
         @pl.loop(chunks - 2, chunks)
         def _(k):
@@ -262,7 +277,6 @@
 
         cotan_copy(d, pair).wait_send()
         cotan_copy(other_d, pair).wait_send()
-        hidden_arrived(d).wait_recv()
 
     @pl.when(inner)
     def _():
@@ -301,15 +315,23 @@
             send_grads(k, half, peer, 0).start()
             send_grads(k, half, pair, 1).start()
             hidden_rows[:, cols] = (silu * up).astype(BF16)
-            for way in range(3):
-                send_hidden(k, way).start()
             hidden_own[:, aligned(d * width + k * LANES, LANES)] = hidden_rows[
                 aligned((r % 2) * block + d * rows, rows), cols
             ]
 
+            @pl.when(k == chunks - 1)
+            def _():
+                send_hidden(0).start()
+
         def spread(k):
             send_grads(k, far, pair, 2).wait_recv()
             send_grads(k, far, pair, 2).start()
+
+            @pl.when(k == chunks - 1)
+            def _():
+                send_hidden(1).start()
+                send_hidden(2).start()
+
             add_tokens_grad(k)
 
         @pl.loop(0, chunks + 2)
@@ -339,6 +361,8 @@
 
     core_copy(1).start()
     core_copy(0).start()
+    turned[...] = tok[...].T
+    keep_tokens().start()
 
     def plane_copy(way):
         where = (
@@ -363,6 +387,10 @@
     ).astype(BF16)
     plane_copy(2).start()
 
+    @pl.when(outer)
+    def _():
+        hidden_arrived(d).wait_recv()
+
     hidden_arrived(other_d).wait_recv()
     hidden_ref[...] = hidden_own[...]
 
@@ -389,8 +417,9 @@
             send_grads(k, half, peer, 0).wait_send()
             send_grads(k, half, pair, 1).wait_send()
             send_grads(k, far, pair, 2).wait_send()
-            for way in range(3):
-                send_hidden(k, way).wait_send()
+
+        for way in range(3):
+            send_hidden(way).wait_send()
 
     keep_tokens().wait()
     pltpu.make_async_copy(grad_gate_ref, grad_gate_ref, out_sem.at[1]).wait()
@@ -417,6 +446,7 @@
     hbm = pl.BlockSpec(memory_space=pl.ANY)
     scratch = [
         pltpu.VMEM((every, feats), BF16),
+        pltpu.VMEM((feats, every), BF16),
         pltpu.VMEM((chunks, feats, 2 * LANES), BF16),
         pltpu.VMEM((chunks, 2, group, 2 * LANES), BF16),
         pltpu.VMEM((chunks, 2, group, 2 * LANES), BF16),
@@ -438,13 +468,14 @@
         dma((2,)),
         dma((4,)),
         dma,
+        dma,
         dma((chunks, 2)),
         dma((chunks, 2)),
         dma((chunks,)),
         dma((chunks,)),
         dma((3, chunks)),
         dma((chunks, 2)),
-        dma((3, chunks)),
+        dma((3,)),
         dma((2,)),
         dma((3,)),
         dma((2,)),
@@ -457,15 +488,15 @@
         out_shape=(
             jax.ShapeDtypeStruct((rows, cols), BF16),
             jax.ShapeDtypeStruct((rows, feats), BF16),
-            jax.ShapeDtypeStruct((every, feats), BF16),
+            jax.ShapeDtypeStruct((feats, every), BF16),
             jax.ShapeDtypeStruct((every, cols // 2), BF16),
             jax.ShapeDtypeStruct((every, cols // 2), BF16),
         ),
-        in_specs=[vmem, hbm, hbm, vmem],
+        in_specs=[hbm, hbm, hbm, hbm],
         out_specs=(vmem, vmem, hbm, hbm, hbm),
         scratch_shapes=scratch,
         compiler_params=pltpu.CompilerParams(
-            collective_id=0, has_side_effects=True, vmem_limit_bytes=44 * 2**20
+            collective_id=0, has_side_effects=True, vmem_limit_bytes=60 * 2**20
         ),
         cost_estimate=pl.CostEstimate(
             flops=8 * every * feats * cols // 2, bytes_accessed=4 * feats * cols,
@@ -474,13 +505,37 @@
     )(tokens, gate_weight, up_weight, grad_hidden)
 
 
+def weight_kernel(tokens_ref, gate_ref, up_ref, gate_out, up_out):
+    tokens = tokens_ref[...]
+    gate_out[...] = jnp.dot(tokens, gate_ref[...], preferred_element_type=F32)
+    up_out[...] = jnp.dot(tokens, up_ref[...], preferred_element_type=F32)
+
+
+def weight_grads(turned_tokens, grad_gate, grad_up):
+    feats, every = turned_tokens.shape
+    cols = grad_gate.shape[1]
+    step = 2 * LANES if cols % (2 * LANES) == 0 else LANES
+    grads = pl.BlockSpec((every, step), lambda at: (0, at))
+    out = pl.BlockSpec((feats, step), lambda at: (0, at))
+    shape = jax.ShapeDtypeStruct((feats, cols), F32)
+    return pl.pallas_call(
+        weight_kernel,
+        grid=(cols // step,),
+        out_shape=(shape, shape),
+        in_specs=[pl.BlockSpec((feats, every), lambda at: (0, 0)), grads, grads],
+        out_specs=(out, out),
+        compiler_params=pltpu.CompilerParams(vmem_limit_bytes=60 * 2**20),
+        cost_estimate=pl.CostEstimate(
+            flops=4 * every * feats * cols, bytes_accessed=8 * feats * cols, transcendentals=0
+        ),
+    )(turned_tokens, grad_gate, grad_up)
+
+
 def on_line(tokens, gate_weight, up_weight, grad_hidden):
-    hidden, grad_tokens, every_tokens, grad_gate, grad_up = exchange(
+    hidden, grad_tokens, turned_tokens, grad_gate, grad_up = exchange(
         tokens, gate_weight, up_weight, grad_hidden
     )
-    grad_gate_weight = jnp.einsum("td,tf->df", every_tokens, grad_gate, preferred_element_type=F32)
-    grad_up_weight = jnp.einsum("td,tf->df", every_tokens, grad_up, preferred_element_type=F32)
-    return (hidden, grad_tokens, grad_gate_weight, grad_up_weight)
+    return (hidden, grad_tokens, *weight_grads(turned_tokens, grad_gate, grad_up))
 
 
 def from_root(value, axis, source):

time: 105 us -> 95.8 us (0.912)
  matrix products: 8.44 us -> 0 us
  local copies, waits for them, and re-layouts: 6.17 us -> 2.27 us
  Pallas kernels: 89.3 us -> 92.5 us
    pallas_call x0 -> x1, Pallas kernels: none -> 8.81 us  [weight_grads(): pl.pallas_call(weight_kernel, grid=(cols // step,), out_shape=(shape, sha...]
    dot_general x2 -> x0, matrix products: 8.44 us -> none  [the longest x1 4.22 us: on_line(): jnp.einsum('td,tf->df', every_tokens, grad_gate, preferred_element_type=F32)]
    pallas_call x1, Pallas kernels: 89.3 us -> 83.7 us  [exchange(): pl.pallas_call(kernel, out_shape=(jax.ShapeDtypeStruct((rows, cols), BF16...]
    unnamed x8 -> x4, local copies, waits for them, and re-layouts: 6.17 us -> 2.27 us
where the time goes in v2:
time: 95.8 us; the launch traced here: 95.5 us
  Pallas kernels  92.5 us (97%)
  local copies, waits for them, and re-layouts  2.27 us (2%)
    pallas_call x1, Pallas kernels, exchange(): pl.pallas_call(kernel, out_shape=(jax.ShapeDtypeStruct((rows, cols), BF16...  83.7 us
    pallas_call x1, Pallas kernels, weight_grads(): pl.pallas_call(weight_kernel, grid=(cols // step,), out_shape=(shape, sha...  8.81 us
    unnamed x4, local copies, waits for them, and re-layouts  2.27 us

profile of v2, /device:TPU:0, one launch (start us, length us, event | category | flops | bytes accessed | tf_op | source)
XLA Modules:
  0.0 95.5 jit_solution(14663199088760436772)
XLA Ops:
  0.6 83.7 %shard_map.75 = (bf16[32,3584]{1,0:T(8,128)(2,1)}, bf16[32,1024]{1,0:T(8,128)(2,1)}, bf16[1024,256]{1,0:T(8,128)(2,1)}, bf16[256,1792]{1,0:T(8,128)(2,1)}, bf16[256,1792]{1,0:T(8,128)(2,1)}) custom-call(bf16[32,1024]{1,0:T(8,128)(2,1)} %tokens_ref.1, bf16[1024,3584]{1,0:T(8,128)(2,1)} %gate_ref.1, bf16[1024,3584]{1,0:T(8,128)(2,1)} %up_ref.1, ...), custom_call_target="tpu_custom_call" | custom-call | flops 3758096384 | bytes 14680064 | tf_op jit(solution)/shard_map/pallas_call | solution.py:486
  84.4 0.0 copy-start
  84.4 8.8 %shard_map.76 = (f32[1024,1792]{1,0:T(8,128)}, f32[1024,1792]{1,0:T(8,128)}) custom-call(bf16[1024,256]{1,0:T(8,128)(2,1)} %get-tuple-element.13.tokens_ref, bf16[256,1792]{1,0:T(8,128)(2,1)} %get-tuple-element.14.gate_ref, bf16[256,1792]{1,0:T(8,128)(2,1)} %get-tuple-element.15.up_ref), custom_call_target="tpu_custom_call" | custom-call | flops 1879048192 | bytes 14680064 | tf_op jit(solution)/shard_map/pallas_call | solution.py:521
  93.2 1.6 %copy.10 = bf16[32,3584]{1,0:T(8,128)(2,1)} copy(bf16[32,3584]{1,0:T(8,128)(2,1)} %get-tuple-element.22) | data formatting | bytes 458752
  94.8 0.0 copy-done
  94.8 0.6 copy.11
Async XLA Ops:
  84.4 10.5 %copy-start = (bf16[32,1024]{1,0:T(8,128)(2,1)S(1)}, bf16[32,1024]{1,0:T(8,128)(2,1)}, u32[]{:S(2)}) copy-start(bf16[32,1024]{1,0:T(8,128)(2,1)} %get-tuple-element.23) | copy-start | bytes 196612

commit v3 on v2

--- a/solution.py
+++ b/solution.py
@@ -243,6 +243,13 @@
             hidden_send.at[0], hidden_recv.at[depth],
         )
 
+    def take_grads(k):
+        send_grads(k, half, r, 0).wait_recv()
+        send_grads(k, far, r, 0).wait_recv()
+        add_tokens_grad(k)
+
+    lag = min(6, chunks)
+
     @pl.when(outer)
     def _():
         @pl.loop(0, chunks)
@@ -263,29 +270,33 @@
             def _():
                 sent[k, half] = partial(k, half).astype(BF16)
                 send_part(k, half).start()
+
+            @pl.when(k >= lag)
+            def _():
+                take_grads(k - lag)
+
+        @pl.loop(chunks - lag, chunks)
+        def _(k):
+            take_grads(k)
 
         @pl.loop(chunks - 2, chunks)
         def _(k):
             send_part(k, far).wait_send()
             send_part(k, half).wait_send()
 
-        @pl.loop(0, chunks)
-        def _(k):
-            send_grads(k, half, r, 0).wait_recv()
-            send_grads(k, far, r, 0).wait_recv()
-            add_tokens_grad(k)
-
         cotan_copy(d, pair).wait_send()
         cotan_copy(other_d, pair).wait_send()
 
     @pl.when(inner)
     def _():
-        def reduce(k):
+        def reduce_far(k):
             weight_wait(k)
             mine = partial(k, far)
             send_part(k, far).wait_recv()
             to_peer[k] = (mine + landed[k, far].astype(F32)).astype(BF16)
             send_peer(k).start()
+
+        def reduce_half(k):
             mine = partial(k, half)
             send_part(k, half).wait_recv()
             own_sum[k] = mine + landed[k, half].astype(F32)
@@ -332,13 +343,11 @@
                 send_hidden(1).start()
                 send_hidden(2).start()
 
-            add_tokens_grad(k)
-
         @pl.loop(0, chunks + 2)
         def _(i):
             @pl.when(i < chunks)
             def _():
-                reduce(i)
+                reduce_far(i)
 
             @pl.when((i >= 1) & (i <= chunks))
             def _():
@@ -347,6 +356,14 @@
             @pl.when(i >= 2)
             def _():
                 spread(i - 2)
+
+            @pl.when(i < chunks)
+            def _():
+                reduce_half(i)
+
+            @pl.when(i >= 2)
+            def _():
+                add_tokens_grad(i - 2)
 
         cotan_copy(other_d, r).wait_send()
 
@@ -505,26 +522,47 @@
     )(tokens, gate_weight, up_weight, grad_hidden)
 
 
-def weight_kernel(tokens_ref, gate_ref, up_ref, gate_out, up_out):
-    tokens = tokens_ref[...]
-    gate_out[...] = jnp.dot(tokens, gate_ref[...], preferred_element_type=F32)
-    up_out[...] = jnp.dot(tokens, up_ref[...], preferred_element_type=F32)
+def weight_kernel(tokens_ref, gate_ref, up_ref, gate_out, up_out, made, sem):
+    cols = gate_ref.shape[1]
+    steps, step = made.shape[1:3]
+    width = 2 * LANES if cols % (2 * LANES) == 0 else LANES
+    pairs = ((gate_ref, gate_out), (up_ref, up_out))
+
+    def leave(at, which):
+        return pltpu.make_async_copy(
+            made.at[which, at], pairs[which][1].at[pl.ds(at * step, step), :], sem.at[which, at]
+        )
+
+    for at in range(steps):
+        tokens = tokens_ref[pl.ds(at * step, step), :]
+        for which in range(2):
+            for col in range(0, cols, width):
+                made[which, at, :, pl.ds(col, width)] = jnp.dot(
+                    tokens, pairs[which][0][:, pl.ds(col, width)], preferred_element_type=F32
+                )
+            leave(at, which).start()
+    for at in range(steps):
+        for which in range(2):
+            leave(at, which).wait()
 
 
 def weight_grads(turned_tokens, grad_gate, grad_up):
     feats, every = turned_tokens.shape
     cols = grad_gate.shape[1]
-    step = 2 * LANES if cols % (2 * LANES) == 0 else LANES
-    grads = pl.BlockSpec((every, step), lambda at: (0, at))
-    out = pl.BlockSpec((feats, step), lambda at: (0, at))
+    steps = 4
     shape = jax.ShapeDtypeStruct((feats, cols), F32)
+    vmem = pl.BlockSpec(memory_space=pltpu.VMEM)
+    hbm = pl.BlockSpec(memory_space=pl.ANY)
     return pl.pallas_call(
         weight_kernel,
-        grid=(cols // step,),
         out_shape=(shape, shape),
-        in_specs=[pl.BlockSpec((feats, every), lambda at: (0, 0)), grads, grads],
-        out_specs=(out, out),
-        compiler_params=pltpu.CompilerParams(vmem_limit_bytes=60 * 2**20),
+        in_specs=[vmem, vmem, vmem],
+        out_specs=(hbm, hbm),
+        scratch_shapes=[
+            pltpu.VMEM((2, steps, feats // steps, cols), F32),
+            pltpu.SemaphoreType.DMA((2, steps)),
+        ],
+        compiler_params=pltpu.CompilerParams(vmem_limit_bytes=28 * 2**20),
         cost_estimate=pl.CostEstimate(
             flops=4 * every * feats * cols, bytes_accessed=8 * feats * cols, transcendentals=0
         ),

time: 95.8 us -> 95.6 us (level)
  Pallas kernels: 92.5 us -> 88.9 us
  local copies, waits for them, and re-layouts: 2.27 us -> 5.67 us
    unnamed x4 -> x10, local copies, waits for them, and re-layouts: 2.27 us -> 5.67 us
    pallas_call x1, Pallas kernels: 8.81 us -> 5.75 us  [weight_grads(): pl.pallas_call(weight_kernel, out_shape=(shape, shape), in_specs=[vmem, v...]
where the time goes in v3:
time: 95.6 us; the launch traced here: 95.2 us
  Pallas kernels  88.9 us (93%)
  local copies, waits for them, and re-layouts  5.67 us (6%)
    pallas_call x1, Pallas kernels, exchange(): pl.pallas_call(kernel, out_shape=(jax.ShapeDtypeStruct((rows, cols), BF16...  83.2 us
    pallas_call x1, Pallas kernels, weight_grads(): pl.pallas_call(weight_kernel, out_shape=(shape, shape), in_specs=[vmem, v...  5.75 us
    unnamed x10, local copies, waits for them, and re-layouts  5.67 us

profile of v3, /device:TPU:0, one launch (start us, length us, event | category | flops | bytes accessed | tf_op | source)
XLA Modules:
  0.0 95.2 jit_solution(13025285316359905961)
XLA Ops:
  0.6 83.2 %shard_map.75 = (bf16[32,3584]{1,0:T(8,128)(2,1)}, bf16[32,1024]{1,0:T(8,128)(2,1)}, bf16[1024,256]{1,0:T(8,128)(2,1)}, bf16[256,1792]{1,0:T(8,128)(2,1)}, bf16[256,1792]{1,0:T(8,128)(2,1)}) custom-call(bf16[32,1024]{1,0:T(8,128)(2,1)} %tokens_ref.1, bf16[1024,3584]{1,0:T(8,128)(2,1)} %gate_ref.1, bf16[1024,3584]{1,0:T(8,128)(2,1)} %up_ref.1, ...), custom_call_target="tpu_custom_call" | custom-call | flops 3758096384 | bytes 14680064 | tf_op jit(solution)/shard_map/pallas_call | solution.py:503
  83.8 0.0 copy-start
  83.8 1.2 %copy-done = bf16[256,1792]{1,0:T(8,128)(2,1)S(1)} copy-done((bf16[256,1792]{1,0:T(8,128)(2,1)S(1)}, bf16[256,1792]{1,0:T(8,128)(2,1)}, u32[]{:S(2)}) %copy-start) | copy-done | bytes 917528
  85.0 0.0 copy-start.1
  85.0 1.2 %copy-done.1 = bf16[256,1792]{1,0:T(8,128)(2,1)S(1)} copy-done((bf16[256,1792]{1,0:T(8,128)(2,1)S(1)}, bf16[256,1792]{1,0:T(8,128)(2,1)}, u32[]{:S(2)}) %copy-start.1) | copy-done | bytes 917528
  86.2 0.0 copy-start.2
  86.2 1.0 %copy-done.2 = bf16[1024,256]{1,0:T(8,128)(2,1)S(1)} copy-done((bf16[1024,256]{1,0:T(8,128)(2,1)S(1)}, bf16[1024,256]{1,0:T(8,128)(2,1)}, u32[]{:S(2)}) %copy-start.2) | copy-done | bytes 524312
  87.2 0.0 copy-start.3
  87.2 5.8 %shard_map.76 = (f32[1024,1792]{1,0:T(8,128)}, f32[1024,1792]{1,0:T(8,128)}) custom-call(bf16[1024,256]{1,0:T(8,128)(2,1)S(1)} %copy-done.2, bf16[256,1792]{1,0:T(8,128)(2,1)S(1)} %copy-done, bf16[256,1792]{1,0:T(8,128)(2,1)S(1)} %copy-done.1), custom_call_target="tpu_custom_call" | custom-call | flops 1879048192 | bytes 14680064 | tf_op jit(solution)/shard_map/pallas_call | solution.py:556
  93.0 1.6 %copy.10 = bf16[32,3584]{1,0:T(8,128)(2,1)} copy(bf16[32,3584]{1,0:T(8,128)(2,1)} %get-tuple-element.22) | data formatting | bytes 458752
  94.6 0.0 copy-done.3
  94.6 0.6 copy.11
Async XLA Ops:
  83.8 1.2 %copy-start = (bf16[256,1792]{1,0:T(8,128)(2,1)S(1)}, bf16[256,1792]{1,0:T(8,128)(2,1)}, u32[]{:S(2)}) copy-start(bf16[256,1792]{1,0:T(8,128)(2,1)} %get-tuple-element.14.gate_ref) | copy-start | bytes 2752516
  85.0 1.2 %copy-start.1 = (bf16[256,1792]{1,0:T(8,128)(2,1)S(1)}, bf16[256,1792]{1,0:T(8,128)(2,1)}, u32[]{:S(2)}) copy-start(bf16[256,1792]{1,0:T(8,128)(2,1)} %get-tuple-element.15.up_ref) | copy-start | bytes 2752516
  86.2 1.0 %copy-start.2 = (bf16[1024,256]{1,0:T(8,128)(2,1)S(1)}, bf16[1024,256]{1,0:T(8,128)(2,1)}, u32[]{:S(2)}) copy-start(bf16[1024,256]{1,0:T(8,128)(2,1)} %get-tuple-element.13.tokens_ref) | copy-start | bytes 1572868
  87.2 7.4 %copy-start.3 = (bf16[32,1024]{1,0:T(8,128)(2,1)S(1)}, bf16[32,1024]{1,0:T(8,128)(2,1)}, u32[]{:S(2)}) copy-start(bf16[32,1024]{1,0:T(8,128)(2,1)} %get-tuple-element.23) | copy-start | bytes 196612

commit v4 on v3

--- a/solution.py
+++ b/solution.py
@@ -19,8 +19,8 @@
 
 def kernel(
     tokens_ref, gate_ref, up_ref, cotan_ref,
-    hidden_ref, grad_tokens_ref, every_tokens_ref, grad_gate_ref, grad_up_ref,
-    tok, turned, weights, sent, landed, to_peer, from_peer, own_sum, grads, cotan, hidden_rows,
+    hidden_ref, grad_tokens_ref, every_tokens_ref, grads_ref,
+    tok, turned, weights, sent, landed, to_peer, from_peer, own_sum, mine, grads, cotan, hidden_rows,
     hidden_own, total, part, core_in, plane_out, plane_in,
     w_sem, tok_send, tok_recv, cotan_send, cotan_recv, cotan_local, own_sem, sent_send, landed_recv,
     peer_send, peer_recv, grads_send, grads_recv, hidden_send, hidden_recv, out_sem,
@@ -157,6 +157,10 @@
             tok[aligned(which * group, group), :], weights[k], preferred_element_type=F32
         )
 
+    def partials(k):
+        both = jnp.dot(tok[...], weights[k], preferred_element_type=F32)
+        return both.reshape(2, group, 2 * LANES)
+
     def weight_wait(k):
         load(k, 0).wait()
         load(k, 1).wait()
@@ -197,26 +201,24 @@
     def keep_tokens():
         return pltpu.make_async_copy(turned, every_tokens_ref, out_sem.at[0])
 
-    def keep(k, which, kind):
-        ref = (grad_gate_ref, grad_up_ref)[kind]
-        return pltpu.make_async_copy(
-            grads.at[k, which, :, pl.ds(kind * LANES, LANES)],
-            ref.at[aligned(which * group, group), aligned(k * LANES, LANES)],
-            out_sem.at[1 + kind],
-        )
+    def keep(k):
+        return pltpu.make_async_copy(grads.at[k], grads_ref.at[k], out_sem.at[1])
 
     def add_tokens_grad(k):
-        for which in range(2):
-            keep(k, which, 0).start()
-            keep(k, which, 1).start()
-        left = grads[k].reshape(2 * group, 2 * LANES)
-        step = min(256, total.shape[1])
-        for at in range(0, total.shape[1], step):
-            term = lax.dot_general(
-                left, weights[k, pl.ds(at, step), :], (((1,), (1,)), ((), ())),
-                preferred_element_type=F32,
-            )
-            total[:, pl.ds(at, step)] += term
+        keep(k).start()
+
+        @pl.when(k % 2 == 1)
+        def _():
+            step = min(256, total.shape[1])
+            for at in range(0, total.shape[1], step):
+                term = jnp.zeros((2 * group, step), F32)
+                for chunk in (k - 1, k):
+                    term += lax.dot_general(
+                        grads[chunk].reshape(2 * group, 2 * LANES),
+                        weights[chunk, pl.ds(at, step), :],
+                        (((1,), (1,)), ((), ())), preferred_element_type=F32,
+                    )
+                total[:, pl.ds(at, step)] += term
 
     total[...] = jnp.zeros_like(total)
 
@@ -263,12 +265,15 @@
                 send_part(k - 2, far).wait_send()
                 send_part(k - 2, half).wait_send()
 
-            sent[k, far] = partial(k, far).astype(BF16)
-            send_part(k, far).start()
+            @pl.when(k == 0)
+            def _():
+                sent[k, far] = partial(k, far).astype(BF16)
+                send_part(k, far).start()
 
             @pl.when(k >= 1)
             def _():
-                sent[k, half] = partial(k, half).astype(BF16)
+                sent[k] = partials(k).astype(BF16)
+                send_part(k, far).start()
                 send_part(k, half).start()
 
             @pl.when(k >= lag)
@@ -289,17 +294,22 @@
 
     @pl.when(inner)
     def _():
+        def prepare(k):
+            weight_wait(k)
+            mine[...] = partials(k)
+
         def reduce_far(k):
-            weight_wait(k)
-            mine = partial(k, far)
             send_part(k, far).wait_recv()
-            to_peer[k] = (mine + landed[k, far].astype(F32)).astype(BF16)
+            to_peer[k] = (mine[far] + landed[k, far].astype(F32)).astype(BF16)
             send_peer(k).start()
 
         def reduce_half(k):
-            mine = partial(k, half)
             send_part(k, half).wait_recv()
-            own_sum[k] = mine + landed[k, half].astype(F32)
+            own_sum[k] = mine[half] + landed[k, half].astype(F32)
+
+            @pl.when(k + 1 < chunks)
+            def _():
+                prepare(k + 1)
 
         def pointwise(k):
             @pl.when(k == 0)
@@ -343,6 +353,8 @@
                 send_hidden(1).start()
                 send_hidden(2).start()
 
+        prepare(0)
+
         @pl.loop(0, chunks + 2)
         def _(i):
             @pl.when(i < chunks)
@@ -439,8 +451,7 @@
             send_hidden(way).wait_send()
 
     keep_tokens().wait()
-    pltpu.make_async_copy(grad_gate_ref, grad_gate_ref, out_sem.at[1]).wait()
-    pltpu.make_async_copy(grad_up_ref, grad_up_ref, out_sem.at[2]).wait()
+    pltpu.make_async_copy(grads, grads_ref, out_sem.at[1]).wait()
     core_copy(0).wait_send()
     core_copy(1).wait_send()
     own = plane_out[0, aligned(d * rows, rows), :].astype(F32)
@@ -470,6 +481,7 @@
         pltpu.VMEM((chunks, group, 2 * LANES), BF16),
         pltpu.VMEM((chunks, group, 2 * LANES), BF16),
         pltpu.VMEM((chunks, group, 2 * LANES), F32),
+        pltpu.VMEM((2, group, 2 * LANES), F32),
         pltpu.VMEM((chunks, 2, group, 2 * LANES), BF16),
         pltpu.VMEM((group, cols // 2), BF16),
         pltpu.VMEM((group, cols // 2), BF16),
@@ -494,7 +506,7 @@
         dma((chunks, 2)),
         dma((3,)),
         dma((2,)),
-        dma((3,)),
+        dma((2,)),
         dma((2,)),
         dma((2,)),
         dma((3,)),
@@ -506,11 +518,10 @@
             jax.ShapeDtypeStruct((rows, cols), BF16),
             jax.ShapeDtypeStruct((rows, feats), BF16),
             jax.ShapeDtypeStruct((feats, every), BF16),
-            jax.ShapeDtypeStruct((every, cols // 2), BF16),
-            jax.ShapeDtypeStruct((every, cols // 2), BF16),
+            jax.ShapeDtypeStruct((chunks, 2, group, 2 * LANES), BF16),
         ),
         in_specs=[hbm, hbm, hbm, hbm],
-        out_specs=(vmem, vmem, hbm, hbm, hbm),
+        out_specs=(vmem, vmem, hbm, hbm),
         scratch_shapes=scratch,
         compiler_params=pltpu.CompilerParams(
             collective_id=0, has_side_effects=True, vmem_limit_bytes=60 * 2**20
@@ -522,58 +533,77 @@
     )(tokens, gate_weight, up_weight, grad_hidden)
 
 
-def weight_kernel(tokens_ref, gate_ref, up_ref, gate_out, up_out, made, sem):
-    cols = gate_ref.shape[1]
+def weight_kernel(
+    tokens_ref, grads_ref, hidden_ref, grad_tokens_ref,
+    hidden_out, grad_tokens_out, gate_out, up_out, made, sem, carry_sem,
+):
+    chunks = grads_ref.shape[0]
     steps, step = made.shape[1:3]
-    width = 2 * LANES if cols % (2 * LANES) == 0 else LANES
-    pairs = ((gate_ref, gate_out), (up_ref, up_out))
+    outs = (gate_out, up_out)
+    carried = (
+        pltpu.make_async_copy(hidden_ref, hidden_out, carry_sem.at[0]),
+        pltpu.make_async_copy(grad_tokens_ref, grad_tokens_out, carry_sem.at[1]),
+    )
 
     def leave(at, which):
         return pltpu.make_async_copy(
-            made.at[which, at], pairs[which][1].at[pl.ds(at * step, step), :], sem.at[which, at]
-        )
-
+            made.at[which, at], outs[which].at[pl.ds(at * step, step), :], sem.at[which, at]
+        )
+
+    for copy in carried:
+        copy.start()
     for at in range(steps):
         tokens = tokens_ref[pl.ds(at * step, step), :]
-        for which in range(2):
-            for col in range(0, cols, width):
-                made[which, at, :, pl.ds(col, width)] = jnp.dot(
-                    tokens, pairs[which][0][:, pl.ds(col, width)], preferred_element_type=F32
-                )
-            leave(at, which).start()
+        for k in range(chunks):
+            both = jnp.dot(
+                tokens, grads_ref[k].reshape(tokens.shape[1], 2 * LANES),
+                preferred_element_type=F32,
+            )
+            made[0, at, :, pl.ds(k * LANES, LANES)] = both[:, :LANES]
+            made[1, at, :, pl.ds(k * LANES, LANES)] = both[:, LANES:]
+        leave(at, 0).start()
+        leave(at, 1).start()
     for at in range(steps):
-        for which in range(2):
-            leave(at, which).wait()
-
-
-def weight_grads(turned_tokens, grad_gate, grad_up):
+        leave(at, 0).wait()
+        leave(at, 1).wait()
+    for copy in carried:
+        copy.wait()
+
+
+def weight_grads(turned_tokens, grads, hidden, grad_tokens):
     feats, every = turned_tokens.shape
-    cols = grad_gate.shape[1]
+    cols = grads.shape[0] * LANES
     steps = 4
     shape = jax.ShapeDtypeStruct((feats, cols), F32)
     vmem = pl.BlockSpec(memory_space=pltpu.VMEM)
     hbm = pl.BlockSpec(memory_space=pl.ANY)
     return pl.pallas_call(
         weight_kernel,
-        out_shape=(shape, shape),
-        in_specs=[vmem, vmem, vmem],
-        out_specs=(hbm, hbm),
+        out_shape=(
+            jax.ShapeDtypeStruct(hidden.shape, hidden.dtype),
+            jax.ShapeDtypeStruct(grad_tokens.shape, grad_tokens.dtype),
+            shape,
+            shape,
+        ),
+        in_specs=[vmem, vmem, hbm, hbm],
+        out_specs=(hbm, hbm, hbm, hbm),
         scratch_shapes=[
             pltpu.VMEM((2, steps, feats // steps, cols), F32),
             pltpu.SemaphoreType.DMA((2, steps)),
+            pltpu.SemaphoreType.DMA((2,)),
         ],
-        compiler_params=pltpu.CompilerParams(vmem_limit_bytes=28 * 2**20),
+        compiler_params=pltpu.CompilerParams(vmem_limit_bytes=60 * 2**20),
         cost_estimate=pl.CostEstimate(
             flops=4 * every * feats * cols, bytes_accessed=8 * feats * cols, transcendentals=0
         ),
-    )(turned_tokens, grad_gate, grad_up)
+    )(turned_tokens, grads, hidden, grad_tokens)
 
 
 def on_line(tokens, gate_weight, up_weight, grad_hidden):
-    hidden, grad_tokens, turned_tokens, grad_gate, grad_up = exchange(
+    hidden, grad_tokens, turned_tokens, grads = exchange(
         tokens, gate_weight, up_weight, grad_hidden
     )
-    return (hidden, grad_tokens, *weight_grads(turned_tokens, grad_gate, grad_up))
+    return weight_grads(turned_tokens, grads, hidden, grad_tokens)
 
 
 def from_root(value, axis, source):
@@ -649,7 +679,7 @@
         (sizes["row"], sizes["col"], sizes["depth"]) == (4, 4, 2)
         and tokens.shape[0] % 16 == 0
         and tokens.shape[1] % 128 == 0
-        and gate_weight.shape[1] % (2 * LANES) == 0
+        and gate_weight.shape[1] % (4 * LANES) == 0
     )
     plan = on_line if fits else local
     return plan(tokens, gate_weight, up_weight, grad_hidden)

time: 95.6 us -> 95.7 us (level)
  Pallas kernels: 88.9 us -> 94.8 us
  local copies, waits for them, and re-layouts: 5.67 us -> 0 us
    pallas_call x1, Pallas kernels: 5.75 us -> 11.8 us  [weight_grads(): pl.pallas_call(weight_kernel, out_shape=(jax.ShapeDtypeStruct(hidden.shap...]
    unnamed x10 -> x0, local copies, waits for them, and re-layouts: 5.67 us -> none
where the time goes in v4:
time: 95.7 us; the launch traced here: 95.5 us
  Pallas kernels  94.8 us (99%)
    pallas_call x1, Pallas kernels, exchange(): pl.pallas_call(kernel, out_shape=(jax.ShapeDtypeStruct((rows, cols), BF16...  83 us
    pallas_call x1, Pallas kernels, weight_grads(): pl.pallas_call(weight_kernel, out_shape=(jax.ShapeDtypeStruct(hidden.shap...  11.8 us

profile of v4, /device:TPU:0, one launch (start us, length us, event | category | flops | bytes accessed | tf_op | source)
XLA Modules:
  0.0 95.5 jit_solution(9327077609933868064)
XLA Ops:
  0.6 83.0 %shard_map.75 = (bf16[32,3584]{1,0:T(8,128)(2,1)}, bf16[32,1024]{1,0:T(8,128)(2,1)}, bf16[1024,256]{1,0:T(8,128)(2,1)}, bf16[14,2,128,256]{3,2,1,0:T(8,128)(2,1)}) custom-call(bf16[32,1024]{1,0:T(8,128)(2,1)} %tokens_ref.1, bf16[1024,3584]{1,0:T(8,128)(2,1)} %gate_ref.1, bf16[1024,3584]{1,0:T(8,128)(2,1)} %up_ref.1, bf16[32,3584]{1,0:T(8,128)(2,1)} %cotan_ref.1), custom_call_target="tpu_custom_call" | custom-call | flops 3758096384 | bytes 14680064 | tf_op jit(solution)/shard_map/pallas_call | solution.py:515
  83.7 11.8 %shard_map.76 = (bf16[32,3584]{1,0:T(8,128)(2,1)}, bf16[32,1024]{1,0:T(8,128)(2,1)}, f32[1024,1792]{1,0:T(8,128)}, f32[1024,1792]{1,0:T(8,128)}) custom-call(bf16[1024,256]{1,0:T(8,128)(2,1)} %get-tuple-element.8.tokens_ref, bf16[14,2,128,256]{3,2,1,0:T(8,128)(2,1)} %get-tuple-element.9.grads_ref, bf16[32,3584]{1,0:T(8,128)(2,1)} %get-tuple-element.10.hidden_ref, ...), custom_call_target="tpu_custom_call" | custom-call | flops 1879048192 | bytes 14680064 | tf_op jit(solution)/shard_map/pallas_call | solution.py:580

commit v5 on v4

--- a/solution.py
+++ b/solution.py
@@ -250,7 +250,9 @@
         send_grads(k, far, r, 0).wait_recv()
         add_tokens_grad(k)
 
-    lag = min(6, chunks)
+    lag = min(12, chunks)
+    flight = min(3, chunks)
+    point_lag, spread_lag = 2, 4
 
     @pl.when(outer)
     def _():
@@ -260,10 +262,10 @@
             def _():
                 weight_wait(k)
 
-            @pl.when(k >= 2)
-            def _():
-                send_part(k - 2, far).wait_send()
-                send_part(k - 2, half).wait_send()
+            @pl.when(k >= flight)
+            def _():
+                send_part(k - flight, far).wait_send()
+                send_part(k - flight, half).wait_send()
 
             @pl.when(k == 0)
             def _():
@@ -284,7 +286,7 @@
         def _(k):
             take_grads(k)
 
-        @pl.loop(chunks - 2, chunks)
+        @pl.loop(chunks - flight, chunks)
         def _(k):
             send_part(k, far).wait_send()
             send_part(k, half).wait_send()
@@ -355,27 +357,24 @@
 
         prepare(0)
 
-        @pl.loop(0, chunks + 2)
+        @pl.loop(0, chunks + spread_lag)
         def _(i):
             @pl.when(i < chunks)
             def _():
                 reduce_far(i)
 
-            @pl.when((i >= 1) & (i <= chunks))
-            def _():
-                pointwise(i - 1)
-
-            @pl.when(i >= 2)
-            def _():
-                spread(i - 2)
+            @pl.when((i >= point_lag) & (i < chunks + point_lag))
+            def _():
+                pointwise(i - point_lag)
 
             @pl.when(i < chunks)
             def _():
                 reduce_half(i)
 
-            @pl.when(i >= 2)
-            def _():
-                add_tokens_grad(i - 2)
+            @pl.when(i >= spread_lag)
+            def _():
+                spread(i - spread_lag)
+                add_tokens_grad(i - spread_lag)
 
         cotan_copy(other_d, r).wait_send()
 
@@ -535,39 +534,70 @@
 
 def weight_kernel(
     tokens_ref, grads_ref, hidden_ref, grad_tokens_ref,
-    hidden_out, grad_tokens_out, gate_out, up_out, made, sem, carry_sem,
+    hidden_out, grad_tokens_out, gate_out, up_out,
+    tokens, grads, hidden, grad_tokens, made, sem, load_sem, grads_sem, carry_sem,
 ):
     chunks = grads_ref.shape[0]
     steps, step = made.shape[1:3]
+    part = step // 2
     outs = (gate_out, up_out)
     carried = (
-        pltpu.make_async_copy(hidden_ref, hidden_out, carry_sem.at[0]),
-        pltpu.make_async_copy(grad_tokens_ref, grad_tokens_out, carry_sem.at[1]),
-    )
-
-    def leave(at, which):
+        (hidden_ref, hidden, hidden_out),
+        (grad_tokens_ref, grad_tokens, grad_tokens_out),
+    )
+
+    def load_tokens(at):
+        rows = pl.ds(at * step, step)
         return pltpu.make_async_copy(
-            made.at[which, at], outs[which].at[pl.ds(at * step, step), :], sem.at[which, at]
-        )
-
-    for copy in carried:
-        copy.start()
+            tokens_ref.at[rows, :], tokens.at[rows, :], load_sem.at[at]
+        )
+
+    def load_grads(k):
+        return pltpu.make_async_copy(grads_ref.at[k], grads.at[k], grads_sem.at[k])
+
+    def carry(which, way):
+        return pltpu.make_async_copy(
+            carried[which][way], carried[which][way + 1], carry_sem.at[way, which]
+        )
+
+    def leave(at, which, piece):
+        return pltpu.make_async_copy(
+            made.at[which, at, pl.ds(piece * part, part), :],
+            outs[which].at[pl.ds(at * step + piece * part, part), :],
+            sem.at[which, at, piece],
+        )
+
+    load_tokens(0).start()
+    for k in range(chunks):
+        load_grads(k).start()
+    for at in range(1, steps):
+        load_tokens(at).start()
+    for which in range(2):
+        carry(which, 0).start()
     for at in range(steps):
-        tokens = tokens_ref[pl.ds(at * step, step), :]
+        load_tokens(at).wait()
+        left = tokens[pl.ds(at * step, step), :]
         for k in range(chunks):
+            if at == 0:
+                load_grads(k).wait()
             both = jnp.dot(
-                tokens, grads_ref[k].reshape(tokens.shape[1], 2 * LANES),
-                preferred_element_type=F32,
+                left, grads[k].reshape(left.shape[1], 2 * LANES), preferred_element_type=F32
             )
             made[0, at, :, pl.ds(k * LANES, LANES)] = both[:, :LANES]
             made[1, at, :, pl.ds(k * LANES, LANES)] = both[:, LANES:]
-        leave(at, 0).start()
-        leave(at, 1).start()
+        for which in range(2):
+            for piece in range(2):
+                leave(at, which, piece).start()
+        if at == 0:
+            for which in range(2):
+                carry(which, 0).wait()
+                carry(which, 1).start()
     for at in range(steps):
-        leave(at, 0).wait()
-        leave(at, 1).wait()
-    for copy in carried:
-        copy.wait()
+        for which in range(2):
+            for piece in range(2):
+                leave(at, which, piece).wait()
+    for which in range(2):
+        carry(which, 1).wait()
 
 
 def weight_grads(turned_tokens, grads, hidden, grad_tokens):
@@ -575,7 +605,6 @@
     cols = grads.shape[0] * LANES
     steps = 4
     shape = jax.ShapeDtypeStruct((feats, cols), F32)
-    vmem = pl.BlockSpec(memory_space=pltpu.VMEM)
     hbm = pl.BlockSpec(memory_space=pl.ANY)
     return pl.pallas_call(
         weight_kernel,
@@ -585,12 +614,18 @@
             shape,
             shape,
         ),
-        in_specs=[vmem, vmem, hbm, hbm],
+        in_specs=[hbm, hbm, hbm, hbm],
         out_specs=(hbm, hbm, hbm, hbm),
         scratch_shapes=[
+            pltpu.VMEM(turned_tokens.shape, BF16),
+            pltpu.VMEM(grads.shape, BF16),
+            pltpu.VMEM(hidden.shape, BF16),
+            pltpu.VMEM(grad_tokens.shape, BF16),
             pltpu.VMEM((2, steps, feats // steps, cols), F32),
-            pltpu.SemaphoreType.DMA((2, steps)),
-            pltpu.SemaphoreType.DMA((2,)),
+            pltpu.SemaphoreType.DMA((2, steps, 2)),
+            pltpu.SemaphoreType.DMA((steps,)),
+            pltpu.SemaphoreType.DMA((grads.shape[0],)),
+            pltpu.SemaphoreType.DMA((2, 2)),
         ],
         compiler_params=pltpu.CompilerParams(vmem_limit_bytes=60 * 2**20),
         cost_estimate=pl.CostEstimate(

time: 95.7 us -> 96.5 us (level)
    pallas_call x1, Pallas kernels: 83 us -> 85.6 us  [exchange(): pl.pallas_call(kernel, out_shape=(jax.ShapeDtypeStruct((rows, cols), BF16...]
    pallas_call x1, Pallas kernels: 11.8 us -> 10.1 us  [weight_grads(): pl.pallas_call(weight_kernel, out_shape=(jax.ShapeDtypeStruct(hidden.shap...]
where the time goes in v5:
time: 96.5 us; the launch traced here: 96.3 us
  Pallas kernels  95.7 us (99%)
    pallas_call x1, Pallas kernels, exchange(): pl.pallas_call(kernel, out_shape=(jax.ShapeDtypeStruct((rows, cols), BF16...  85.6 us
    pallas_call x1, Pallas kernels, weight_grads(): pl.pallas_call(weight_kernel, out_shape=(jax.ShapeDtypeStruct(hidden.shap...  10.1 us

profile of v5, /device:TPU:0, one launch (start us, length us, event | category | flops | bytes accessed | tf_op | source)
XLA Modules:
  0.0 96.3 jit_solution(7452179527973690130)
XLA Ops:
  0.6 85.6 %shard_map.75 = (bf16[32,3584]{1,0:T(8,128)(2,1)}, bf16[32,1024]{1,0:T(8,128)(2,1)}, bf16[1024,256]{1,0:T(8,128)(2,1)}, bf16[14,2,128,256]{3,2,1,0:T(8,128)(2,1)}) custom-call(bf16[32,1024]{1,0:T(8,128)(2,1)} %tokens_ref.1, bf16[1024,3584]{1,0:T(8,128)(2,1)} %gate_ref.1, bf16[1024,3584]{1,0:T(8,128)(2,1)} %up_ref.1, bf16[32,3584]{1,0:T(8,128)(2,1)} %cotan_ref.1), custom_call_target="tpu_custom_call" | custom-call | flops 3758096384 | bytes 14680064 | tf_op jit(solution)/shard_map/pallas_call | solution.py:514
  86.3 10.1 %shard_map.76 = (bf16[32,3584]{1,0:T(8,128)(2,1)}, bf16[32,1024]{1,0:T(8,128)(2,1)}, f32[1024,1792]{1,0:T(8,128)}, f32[1024,1792]{1,0:T(8,128)}) custom-call(bf16[1024,256]{1,0:T(8,128)(2,1)} %get-tuple-element.8.tokens_ref, bf16[14,2,128,256]{3,2,1,0:T(8,128)(2,1)} %get-tuple-element.9.grads_ref, bf16[32,3584]{1,0:T(8,128)(2,1)} %get-tuple-element.10.hidden_ref, ...), custom_call_target="tpu_custom_call" | custom-call | flops 1879048192 | bytes 14680064 | tf_op jit(solution)/shard_map/pallas_call | solution.py:609

commit v6 on v5

--- a/solution.py
+++ b/solution.py
@@ -19,7 +19,7 @@
 
 def kernel(
     tokens_ref, gate_ref, up_ref, cotan_ref,
-    hidden_ref, grad_tokens_ref, every_tokens_ref, grads_ref,
+    hidden_ref, grad_tokens_ref, every_tokens_ref, grad_gate_ref, grad_up_ref,
     tok, turned, weights, sent, landed, to_peer, from_peer, own_sum, mine, grads, cotan, hidden_rows,
     hidden_own, total, part, core_in, plane_out, plane_in,
     w_sem, tok_send, tok_recv, cotan_send, cotan_recv, cotan_local, own_sem, sent_send, landed_recv,
@@ -117,6 +117,16 @@
     def _():
         first_hop().start()
 
+    @pl.when(outer)
+    def _():
+        cotan_copy(d, pair).start()
+        cotan_copy(other_d, pair).start()
+
+    @pl.when(inner)
+    def _():
+        own_cotan().start()
+        cotan_copy(other_d, r).start()
+
     @pl.when(is_root)
     def _():
         own_tokens().start()
@@ -174,16 +184,6 @@
     near(0)
     near(1)
 
-    @pl.when(outer)
-    def _():
-        cotan_copy(d, pair).start()
-        cotan_copy(other_d, pair).start()
-
-    @pl.when(inner)
-    def _():
-        own_cotan().start()
-        cotan_copy(other_d, r).start()
-
     away(0)
     away(1)
 
@@ -201,11 +201,18 @@
     def keep_tokens():
         return pltpu.make_async_copy(turned, every_tokens_ref, out_sem.at[0])
 
-    def keep(k):
-        return pltpu.make_async_copy(grads.at[k], grads_ref.at[k], out_sem.at[1])
+    def keep(k, which, kind):
+        ref = (grad_gate_ref, grad_up_ref)[kind]
+        return pltpu.make_async_copy(
+            grads.at[k, which, :, pl.ds(kind * LANES, LANES)],
+            ref.at[aligned(which * group, group), aligned(k * LANES, LANES)],
+            out_sem.at[1 + kind],
+        )
 
     def add_tokens_grad(k):
-        keep(k).start()
+        for which in range(2):
+            keep(k, which, 0).start()
+            keep(k, which, 1).start()
 
         @pl.when(k % 2 == 1)
         def _():
@@ -250,9 +257,8 @@
         send_grads(k, far, r, 0).wait_recv()
         add_tokens_grad(k)
 
-    lag = min(12, chunks)
-    flight = min(3, chunks)
-    point_lag, spread_lag = 2, 4
+    lag = min(8, chunks)
+    flight = min(2, chunks)
 
     @pl.when(outer)
     def _():
@@ -357,24 +363,27 @@
 
         prepare(0)
 
-        @pl.loop(0, chunks + spread_lag)
+        @pl.loop(0, chunks + 2)
         def _(i):
             @pl.when(i < chunks)
             def _():
                 reduce_far(i)
 
-            @pl.when((i >= point_lag) & (i < chunks + point_lag))
-            def _():
-                pointwise(i - point_lag)
+            @pl.when((i >= 1) & (i <= chunks))
+            def _():
+                pointwise(i - 1)
+
+            @pl.when(i >= 2)
+            def _():
+                spread(i - 2)
 
             @pl.when(i < chunks)
             def _():
                 reduce_half(i)
 
-            @pl.when(i >= spread_lag)
-            def _():
-                spread(i - spread_lag)
-                add_tokens_grad(i - spread_lag)
+            @pl.when(i >= 2)
+            def _():
+                add_tokens_grad(i - 2)
 
         cotan_copy(other_d, r).wait_send()
 
@@ -450,7 +459,8 @@
             send_hidden(way).wait_send()
 
     keep_tokens().wait()
-    pltpu.make_async_copy(grads, grads_ref, out_sem.at[1]).wait()
+    pltpu.make_async_copy(grad_gate_ref, grad_gate_ref, out_sem.at[1]).wait()
+    pltpu.make_async_copy(grad_up_ref, grad_up_ref, out_sem.at[2]).wait()
     core_copy(0).wait_send()
     core_copy(1).wait_send()
     own = plane_out[0, aligned(d * rows, rows), :].astype(F32)
@@ -505,7 +515,7 @@
         dma((chunks, 2)),
         dma((3,)),
         dma((2,)),
-        dma((2,)),
+        dma((3,)),
         dma((2,)),
         dma((2,)),
         dma((3,)),
@@ -517,10 +527,11 @@
             jax.ShapeDtypeStruct((rows, cols), BF16),
             jax.ShapeDtypeStruct((rows, feats), BF16),
             jax.ShapeDtypeStruct((feats, every), BF16),
-            jax.ShapeDtypeStruct((chunks, 2, group, 2 * LANES), BF16),
+            jax.ShapeDtypeStruct((every, cols // 2), BF16),
+            jax.ShapeDtypeStruct((every, cols // 2), BF16),
         ),
         in_specs=[hbm, hbm, hbm, hbm],
-        out_specs=(vmem, vmem, hbm, hbm),
+        out_specs=(vmem, vmem, hbm, hbm, hbm),
         scratch_shapes=scratch,
         compiler_params=pltpu.CompilerParams(
             collective_id=0, has_side_effects=True, vmem_limit_bytes=60 * 2**20
@@ -533,11 +544,12 @@
 
 
 def weight_kernel(
-    tokens_ref, grads_ref, hidden_ref, grad_tokens_ref,
+    tokens_ref, gate_ref, up_ref, hidden_ref, grad_tokens_ref,
     hidden_out, grad_tokens_out, gate_out, up_out,
-    tokens, grads, hidden, grad_tokens, made, sem, load_sem, grads_sem, carry_sem,
+    tokens, gate, up, hidden, grad_tokens, made, sem, load_sem, grads_sem, carry_sem,
 ):
-    chunks = grads_ref.shape[0]
+    width = 2 * LANES
+    tiles = gate.shape[1] // width
     steps, step = made.shape[1:3]
     part = step // 2
     outs = (gate_out, up_out)
@@ -552,8 +564,12 @@
             tokens_ref.at[rows, :], tokens.at[rows, :], load_sem.at[at]
         )
 
-    def load_grads(k):
-        return pltpu.make_async_copy(grads_ref.at[k], grads.at[k], grads_sem.at[k])
+    def load_grads(which, at):
+        cols = pl.ds(at * width, width)
+        source, held = ((gate_ref, gate), (up_ref, up))[which]
+        return pltpu.make_async_copy(
+            source.at[:, cols], held.at[:, cols], grads_sem.at[which, at]
+        )
 
     def carry(which, way):
         return pltpu.make_async_copy(
@@ -568,8 +584,9 @@
         )
 
     load_tokens(0).start()
-    for k in range(chunks):
-        load_grads(k).start()
+    for which in range(2):
+        for tile in range(tiles):
+            load_grads(which, tile).start()
     for at in range(1, steps):
         load_tokens(at).start()
     for which in range(2):
@@ -577,15 +594,14 @@
     for at in range(steps):
         load_tokens(at).wait()
         left = tokens[pl.ds(at * step, step), :]
-        for k in range(chunks):
-            if at == 0:
-                load_grads(k).wait()
-            both = jnp.dot(
-                left, grads[k].reshape(left.shape[1], 2 * LANES), preferred_element_type=F32
-            )
-            made[0, at, :, pl.ds(k * LANES, LANES)] = both[:, :LANES]
-            made[1, at, :, pl.ds(k * LANES, LANES)] = both[:, LANES:]
         for which in range(2):
+            for tile in range(tiles):
+                if at == 0:
+                    load_grads(which, tile).wait()
+                cols = pl.ds(tile * width, width)
+                made[which, at, :, cols] = jnp.dot(
+                    left, (gate, up)[which][:, cols], preferred_element_type=F32
+                )
             for piece in range(2):
                 leave(at, which, piece).start()
         if at == 0:
@@ -600,9 +616,9 @@
         carry(which, 1).wait()
 
 
-def weight_grads(turned_tokens, grads, hidden, grad_tokens):
+def weight_grads(turned_tokens, grad_gate, grad_up, hidden, grad_tokens):
     feats, every = turned_tokens.shape
-    cols = grads.shape[0] * LANES
+    cols = grad_gate.shape[1]
     steps = 4
     shape = jax.ShapeDtypeStruct((feats, cols), F32)
     hbm = pl.BlockSpec(memory_space=pl.ANY)
@@ -614,31 +630,32 @@
             shape,
             shape,
         ),
-        in_specs=[hbm, hbm, hbm, hbm],
+        in_specs=[hbm, hbm, hbm, hbm, hbm],
         out_specs=(hbm, hbm, hbm, hbm),
         scratch_shapes=[
             pltpu.VMEM(turned_tokens.shape, BF16),
-            pltpu.VMEM(grads.shape, BF16),
+            pltpu.VMEM(grad_gate.shape, BF16),
+            pltpu.VMEM(grad_up.shape, BF16),
             pltpu.VMEM(hidden.shape, BF16),
             pltpu.VMEM(grad_tokens.shape, BF16),
             pltpu.VMEM((2, steps, feats // steps, cols), F32),
             pltpu.SemaphoreType.DMA((2, steps, 2)),
             pltpu.SemaphoreType.DMA((steps,)),
-            pltpu.SemaphoreType.DMA((grads.shape[0],)),
+            pltpu.SemaphoreType.DMA((2, cols // (2 * LANES))),
             pltpu.SemaphoreType.DMA((2, 2)),
         ],
         compiler_params=pltpu.CompilerParams(vmem_limit_bytes=60 * 2**20),
         cost_estimate=pl.CostEstimate(
             flops=4 * every * feats * cols, bytes_accessed=8 * feats * cols, transcendentals=0
         ),
-    )(turned_tokens, grads, hidden, grad_tokens)
+    )(turned_tokens, grad_gate, grad_up, hidden, grad_tokens)
 
 
 def on_line(tokens, gate_weight, up_weight, grad_hidden):
-    hidden, grad_tokens, turned_tokens, grads = exchange(
+    hidden, grad_tokens, turned_tokens, grad_gate, grad_up = exchange(
         tokens, gate_weight, up_weight, grad_hidden
     )
-    return weight_grads(turned_tokens, grads, hidden, grad_tokens)
+    return weight_grads(turned_tokens, grad_gate, grad_up, hidden, grad_tokens)
 
 
 def from_root(value, axis, source):

time: 96.5 us -> 93.4 us (0.968)
  Pallas kernels: 95.7 us -> 92.6 us
    pallas_call x1, Pallas kernels: 85.6 us -> 83.1 us  [exchange(): pl.pallas_call(kernel, out_shape=(jax.ShapeDtypeStruct((rows, cols), BF16...]
where the time goes in v6:
time: 93.4 us; the launch traced here: 93.2 us
  Pallas kernels  92.6 us (99%)
    pallas_call x1, Pallas kernels, exchange(): pl.pallas_call(kernel, out_shape=(jax.ShapeDtypeStruct((rows, cols), BF16...  83.1 us
    pallas_call x1, Pallas kernels, weight_grads(): pl.pallas_call(weight_kernel, out_shape=(jax.ShapeDtypeStruct(hidden.shap...  9.53 us

profile of v6, /device:TPU:0, one launch (start us, length us, event | category | flops | bytes accessed | tf_op | source)
XLA Modules:
  0.0 93.2 jit_solution(4122614572744536774)
XLA Ops:
  0.6 83.1 %shard_map.75 = (bf16[32,3584]{1,0:T(8,128)(2,1)}, bf16[32,1024]{1,0:T(8,128)(2,1)}, bf16[1024,256]{1,0:T(8,128)(2,1)}, bf16[256,1792]{1,0:T(8,128)(2,1)}, bf16[256,1792]{1,0:T(8,128)(2,1)}) custom-call(bf16[32,1024]{1,0:T(8,128)(2,1)} %tokens_ref.1, bf16[1024,3584]{1,0:T(8,128)(2,1)} %gate_ref.1, bf16[1024,3584]{1,0:T(8,128)(2,1)} %up_ref.1, ...), custom_call_target="tpu_custom_call" | custom-call | flops 3758096384 | bytes 14680064 | tf_op jit(solution)/shard_map/pallas_call | solution.py:524
  83.7 9.5 %shard_map.76 = (bf16[32,3584]{1,0:T(8,128)(2,1)}, bf16[32,1024]{1,0:T(8,128)(2,1)}, f32[1024,1792]{1,0:T(8,128)}, f32[1024,1792]{1,0:T(8,128)}) custom-call(bf16[1024,256]{1,0:T(8,128)(2,1)} %get-tuple-element.9.tokens_ref, bf16[256,1792]{1,0:T(8,128)(2,1)} %get-tuple-element.10.gate_ref, bf16[256,1792]{1,0:T(8,128)(2,1)} %get-tuple-element.11.up_ref, ...), custom_call_target="tpu_custom_call" | custom-call | flops 1879048192 | bytes 14680064 | tf_op jit(solution)/shard_map/pallas_call | solution.py:625

commit v7 on v6

--- a/solution.py
+++ b/solution.py
@@ -54,11 +54,6 @@
             w_sem.at[which, k],
         )
 
-    @pl.loop(0, chunks)
-    def _(k):
-        load(k, 0).start()
-        load(k, 1).start()
-
     barrier = pltpu.get_barrier_semaphore()
     partners = [dict(row=(r + step) % 4) for step in (1, 2, 3)] + [
         dict(row=pair, depth=other_d),
@@ -72,6 +67,11 @@
             barrier, inc=1, device_id={"row": r, "col": c, "depth": d, **where},
             device_id_type=MESH,
         )
+    @pl.loop(0, chunks)
+    def _(k):
+        load(k, 0).start()
+        load(k, 1).start()
+
     pl.semaphore_wait(barrier, len(partners))
 
     def piece(row, depth):
@@ -213,6 +213,11 @@
         for which in range(2):
             keep(k, which, 0).start()
             keep(k, which, 1).start()
+
+        @pl.when(k == chunks // 2)
+        def _():
+            turned[...] = tok[...].T
+            keep_tokens().start()
 
         @pl.when(k % 2 == 1)
         def _():
@@ -356,11 +361,6 @@
             send_grads(k, far, pair, 2).wait_recv()
             send_grads(k, far, pair, 2).start()
 
-            @pl.when(k == chunks - 1)
-            def _():
-                send_hidden(1).start()
-                send_hidden(2).start()
-
         prepare(0)
 
         @pl.loop(0, chunks + 2)
@@ -385,6 +385,9 @@
             def _():
                 add_tokens_grad(i - 2)
 
+        send_grads(chunks - 1, far, pair, 2).wait_send()
+        send_hidden(1).start()
+        send_hidden(2).start()
         cotan_copy(other_d, r).wait_send()
 
     part[...] = total[...].astype(BF16)
@@ -398,8 +401,6 @@
 
     core_copy(1).start()
     core_copy(0).start()
-    turned[...] = tok[...].T
-    keep_tokens().start()
 
     def plane_copy(way):
         where = (
@@ -453,7 +454,10 @@
             send_peer(k).wait_send()
             send_grads(k, half, peer, 0).wait_send()
             send_grads(k, half, pair, 1).wait_send()
-            send_grads(k, far, pair, 2).wait_send()
+
+            @pl.when(k < chunks - 1)
+            def _():
+                send_grads(k, far, pair, 2).wait_send()
 
         for way in range(3):
             send_hidden(way).wait_send()

time: 93.4 us -> 92.9 us (level)
  no operation moved by 1% of the time
where the time goes in v7:
time: 92.9 us; the launch traced here: 92.7 us
  Pallas kernels  92.1 us (99%)
    pallas_call x1, Pallas kernels, exchange(): pl.pallas_call(kernel, out_shape=(jax.ShapeDtypeStruct((rows, cols), BF16...  82.6 us
    pallas_call x1, Pallas kernels, weight_grads(): pl.pallas_call(weight_kernel, out_shape=(jax.ShapeDtypeStruct(hidden.shap...  9.53 us

profile of v7, /device:TPU:0, one launch (start us, length us, event | category | flops | bytes accessed | tf_op | source)
XLA Modules:
  0.0 92.7 jit_solution(7484654403442214244)
XLA Ops:
  0.6 82.6 %shard_map.75 = (bf16[32,3584]{1,0:T(8,128)(2,1)}, bf16[32,1024]{1,0:T(8,128)(2,1)}, bf16[1024,256]{1,0:T(8,128)(2,1)}, bf16[256,1792]{1,0:T(8,128)(2,1)}, bf16[256,1792]{1,0:T(8,128)(2,1)}) custom-call(bf16[32,1024]{1,0:T(8,128)(2,1)} %tokens_ref.1, bf16[1024,3584]{1,0:T(8,128)(2,1)} %gate_ref.1, bf16[1024,3584]{1,0:T(8,128)(2,1)} %up_ref.1, ...), custom_call_target="tpu_custom_call" | custom-call | flops 3758096384 | bytes 14680064 | tf_op jit(solution)/shard_map/pallas_call | solution.py:528
  83.2 9.5 %shard_map.76 = (bf16[32,3584]{1,0:T(8,128)(2,1)}, bf16[32,1024]{1,0:T(8,128)(2,1)}, f32[1024,1792]{1,0:T(8,128)}, f32[1024,1792]{1,0:T(8,128)}) custom-call(bf16[1024,256]{1,0:T(8,128)(2,1)} %get-tuple-element.9.tokens_ref, bf16[256,1792]{1,0:T(8,128)(2,1)} %get-tuple-element.10.gate_ref, bf16[256,1792]{1,0:T(8,128)(2,1)} %get-tuple-element.11.up_ref, ...), custom_call_target="tpu_custom_call" | custom-call | flops 1879048192 | bytes 14680064 | tf_op jit(solution)/shard_map/pallas_call | solution.py:629

commit v8 on v7

--- a/solution.py
+++ b/solution.py
@@ -599,13 +599,12 @@
         load_tokens(at).wait()
         left = tokens[pl.ds(at * step, step), :]
         for which in range(2):
-            for tile in range(tiles):
-                if at == 0:
+            if at == 0:
+                for tile in range(tiles):
                     load_grads(which, tile).wait()
-                cols = pl.ds(tile * width, width)
-                made[which, at, :, cols] = jnp.dot(
-                    left, (gate, up)[which][:, cols], preferred_element_type=F32
-                )
+            made[which, at] = jnp.dot(
+                left, (gate, up)[which][...], preferred_element_type=F32
+            )
             for piece in range(2):
                 leave(at, which, piece).start()
         if at == 0:

time: 92.9 us -> 90.9 us (0.978)
  Pallas kernels: 92.1 us -> 90.1 us
    pallas_call x1, Pallas kernels: 9.53 us -> 7.5 us  [weight_grads(): pl.pallas_call(weight_kernel, out_shape=(jax.ShapeDtypeStruct(hidden.shap...]
where the time goes in v8:
time: 90.9 us; the launch traced here: 90.7 us
  Pallas kernels  90.1 us (99%)
    pallas_call x1, Pallas kernels, exchange(): pl.pallas_call(kernel, out_shape=(jax.ShapeDtypeStruct((rows, cols), BF16...  82.6 us
    pallas_call x1, Pallas kernels, weight_grads(): pl.pallas_call(weight_kernel, out_shape=(jax.ShapeDtypeStruct(hidden.shap...  7.5 us

profile of v8, /device:TPU:0, one launch (start us, length us, event | category | flops | bytes accessed | tf_op | source)
XLA Modules:
  0.0 90.7 jit_solution(6816629805495715328)
XLA Ops:
  0.6 82.6 %shard_map.75 = (bf16[32,3584]{1,0:T(8,128)(2,1)}, bf16[32,1024]{1,0:T(8,128)(2,1)}, bf16[1024,256]{1,0:T(8,128)(2,1)}, bf16[256,1792]{1,0:T(8,128)(2,1)}, bf16[256,1792]{1,0:T(8,128)(2,1)}) custom-call(bf16[32,1024]{1,0:T(8,128)(2,1)} %tokens_ref.1, bf16[1024,3584]{1,0:T(8,128)(2,1)} %gate_ref.1, bf16[1024,3584]{1,0:T(8,128)(2,1)} %up_ref.1, ...), custom_call_target="tpu_custom_call" | custom-call | flops 3758096384 | bytes 14680064 | tf_op jit(solution)/shard_map/pallas_call | solution.py:528
  83.2 7.5 %shard_map.76 = (bf16[32,3584]{1,0:T(8,128)(2,1)}, bf16[32,1024]{1,0:T(8,128)(2,1)}, f32[1024,1792]{1,0:T(8,128)}, f32[1024,1792]{1,0:T(8,128)}) custom-call(bf16[1024,256]{1,0:T(8,128)(2,1)} %get-tuple-element.9.tokens_ref, bf16[256,1792]{1,0:T(8,128)(2,1)} %get-tuple-element.10.gate_ref, bf16[256,1792]{1,0:T(8,128)(2,1)} %get-tuple-element.11.up_ref, ...), custom_call_target="tpu_custom_call" | custom-call | flops 1879048192 | bytes 14680064 | tf_op jit(solution)/shard_map/pallas_call | solution.py:628
